TPU v7x, 256 devices: a whole 4x4x8 slice. The times are simulated.
256 devices in a mesh: section: 2 (over core), gx: 16 (over y, x), dp: 8 (over z).
Axes of the slice: x: 4, y: 4, z: 8, core: 2. Of those that a mesh axis runs over, the one named last changes fastest.
Arguments:
- fields: float32 [16, 8, 64, 8, 128], P('dp', None, 'gx'), may hold values from -6 to 6
- targets: float32 [16, 8, 64, 8, 128], P('dp', None, 'gx'), may hold values from -6 to 6
- weight_in: float32 [8, 64, 56], P('section'), may hold values from -0.75 to 0.75
- bias_in: float32 [8, 64], replicated, may hold values from -3 to 3
- weight_out: float32 [8, 8, 64], P('section'), may hold values from -0.75 to 0.75
- batch_order: int32 [2], replicated, may hold values from 0 to 1, each once
Outputs:
- grad_weight_in: float32 [8, 64, 56], P('section')
- grad_bias_in: float32 [8, 64], P('section')
- grad_weight_out: float32 [8, 8, 64], P('section')
Inputs may be any that keep to these rules, and one draw needn't show every extreme that they name: `batch_order`: each of 0 to 1 appears once.
All inputs are finite; a program needn't handle non-finite values.
Results may differ from a plain program's by a relative error of at most 0.0042.
Values may be sent and summed in bfloat16 or wider, within the bound.
No kernel may reach another device: no remote copies, remote signals or barrier semaphores. Data moves between devices by JAX's collectives and lax.ppermute only.
A program may use at most 64 MiB of HBM per device.

v0:
```python
from functools import partial
import math

import jax
import jax.numpy as jnp
from jax import lax
from jax.sharding import PartitionSpec as P

CORRECTION_GAIN = 0.1
LOSS_GAIN = 8.0
SPEED_X = 0.2
DIFFUSE_X = 0.25
SPEED_Y = 0.15
SPEED_Z = 0.1


def with_halo(shard, sides, width):
    for axis, dim in sides:
        devices, length = (lax.axis_size(axis), shard.shape[dim])
        up = [(i, (i + 1) % devices) for i in range(devices)]
        down = [(j, i) for i, j in up]
        last = lax.slice_in_dim(shard, length - width, length, axis=dim)
        initial = lax.slice_in_dim(shard, 0, width, axis=dim)
        before = lax.ppermute(last, axis, up)
        after = lax.ppermute(initial, axis, down)
        shard = jnp.concatenate([before, shard, after], axis=dim)
    return shard


def for_sending(shard):
    return jax.tree.map(lambda a: a.astype(jnp.bfloat16) if a.dtype == jnp.float32 else a, shard)


def shifted(block, axis, distance):
    devices = range(lax.axis_size(axis))
    route = [(i - distance, i) for i in devices if i - distance in devices]
    return lax.ppermute(block, axis, route)


def neighbours(field, axis):
    return (jnp.roll(field, 1, axis), jnp.roll(field, -1, axis))


def back_neighbours(minus_cot, plus_cot, axis):
    return jnp.roll(minus_cot, -1, axis) + jnp.roll(plus_cot, 1, axis)


def features(padded):
    centre = padded[:, 1:-1]
    x_minus = padded[:, :-2]
    x_plus = padded[:, 2:]
    y_minus, y_plus = neighbours(centre, 2)
    z_minus, z_plus = neighbours(centre, 3)
    channels, rows_x, rows_y, rows_z = centre.shape
    stacked = jnp.stack([centre, x_minus, x_plus, y_minus, y_plus, z_minus, z_plus])
    stacked = stacked.reshape(7 * channels, rows_x * rows_y * rows_z).astype(jnp.bfloat16)
    return (centre, x_minus, x_plus, y_minus, z_minus, stacked)


def advance(padded, weight_in, bias_in, weight_out):
    centre, x_minus, x_plus, y_minus, z_minus, stacked = features(padded)
    act = jnp.tanh(
        jnp.dot(weight_in.astype(jnp.bfloat16), stacked, preferred_element_type=jnp.float32)
        + bias_in[:, None]
    )
    hidden = act.astype(jnp.bfloat16)
    correction = jnp.dot(
        weight_out.astype(jnp.bfloat16), hidden, preferred_element_type=jnp.float32
    ).reshape(centre.shape)
    return (
        centre
        - SPEED_X * (centre - x_minus)
        + DIFFUSE_X * (x_plus - 2.0 * centre + x_minus)
        - SPEED_Y * (centre - y_minus)
        - SPEED_Z * (centre - z_minus)
        + CORRECTION_GAIN * correction
    )


def retreat(padded, cotangent, weight_in, bias_in, weight_out):
    centre, x_minus, x_plus, y_minus, z_minus, stacked = features(padded)
    channels, rows_x, rows_y, rows_z = centre.shape
    cell_count = rows_x * rows_y * rows_z
    w_in = weight_in.astype(jnp.bfloat16)
    w_out = weight_out.astype(jnp.bfloat16)
    act = jnp.tanh(jnp.dot(w_in, stacked, preferred_element_type=jnp.float32) + bias_in[:, None])
    hidden = act.astype(jnp.bfloat16)
    cot_corr = (CORRECTION_GAIN * cotangent).reshape(channels, cell_count).astype(jnp.bfloat16)
    grad_out = jnp.dot(cot_corr, hidden.T, preferred_element_type=jnp.float32)
    cot_pre = jnp.dot(w_out.T, cot_corr, preferred_element_type=jnp.float32) * (1.0 - act * act)
    grad_bias = jnp.sum(cot_pre, axis=1)
    cot_pre_half = cot_pre.astype(jnp.bfloat16)
    grad_in = jnp.dot(cot_pre_half, stacked.T, preferred_element_type=jnp.float32)
    cot_stack = jnp.dot(w_in.T, cot_pre_half, preferred_element_type=jnp.float32)
    cot_stack = cot_stack.reshape(7, channels, rows_x, rows_y, rows_z)
    keep = 1.0 - SPEED_X - 2.0 * DIFFUSE_X - SPEED_Y - SPEED_Z
    cot_centre = keep * cotangent + cot_stack[0]
    cot_centre = cot_centre + back_neighbours(cot_stack[3] + SPEED_Y * cotangent, cot_stack[4], 2)
    cot_centre = cot_centre + back_neighbours(cot_stack[5] + SPEED_Z * cotangent, cot_stack[6], 3)
    cot_below = cot_stack[1] + (SPEED_X + DIFFUSE_X) * cotangent
    cot_above = cot_stack[2] + DIFFUSE_X * cotangent
    zero_row = jnp.zeros_like(cotangent[:, :1])
    pad_cot = jnp.concatenate([zero_row, cot_centre, zero_row], axis=1)
    pad_cot = pad_cot + jnp.concatenate([cot_below, zero_row, zero_row], axis=1)
    pad_cot = pad_cot + jnp.concatenate([zero_row, zero_row, cot_above], axis=1)
    return (pad_cot, grad_in, grad_bias, grad_out)


def body(fields, targets, weight_in, bias_in, weight_out, batch_order):
    section_count = lax.axis_size("section")
    section_index = lax.axis_index("section")
    members, channels, slab_rows, rows_y, rows_z = fields.shape
    grid_rows = slab_rows * lax.axis_size("gx")
    cell_count = members * lax.axis_size("dp") * channels * grid_rows * rows_y * rows_z
    loss_scale = LOSS_GAIN / math.sqrt(cell_count)
    block = weight_in.shape[0]
    zero_in = jnp.zeros(weight_in.shape[1:], jnp.float32)
    zero_bias = jnp.zeros(bias_in.shape[1:], jnp.float32)
    zero_out = jnp.zeros(weight_out.shape[1:], jnp.float32)
    local_bias = lax.dynamic_slice_in_dim(bias_in, section_index * block, block, 0)
    local_weights = (weight_in, local_bias, weight_out)

    def layer_step(padded, layer, weights):
        return advance(padded, weights[0][layer], weights[1][layer], weights[2][layer])

    def layer_back(padded, cotangent, layer, weights):
        return retreat(padded, cotangent, weights[0][layer], weights[1][layer], weights[2][layer])

    def spare_step(padded):
        return padded[:, 1:-1] * 0.0

    def spare_back(padded, cotangent):
        return (padded * 0.0, zero_in, zero_bias, zero_out)

    def thin_ghosts(current):
        return with_halo(current.astype(jnp.bfloat16), (("gx", 1),), 1).astype(current.dtype)

    def run_forward(current, active, weights):
        depth = weights[0].shape[0]
        for layer in range(depth):
            padded = thin_ghosts(current)
            current = lax.cond(
                active, partial(layer_step, layer=layer, weights=weights), spare_step, padded
            )
        return current

    def run_backward(current, cotangent, active, weights):
        depth = weights[0].shape[0]
        saved_pads = []
        for layer in range(depth):
            padded = thin_ghosts(current)
            saved_pads.append(padded)
            current = lax.cond(
                active, partial(layer_step, layer=layer, weights=weights), spare_step, padded
            )
        grads_in = [zero_in] * depth
        grads_bias = [zero_bias] * depth
        grads_out = [zero_out] * depth
        for layer in reversed(range(depth)):
            pad_cot, grads_in[layer], grads_bias[layer], grads_out[layer] = lax.cond(
                active,
                partial(layer_back, layer=layer, weights=weights),
                spare_back,
                saved_pads[layer],
                cotangent,
            )
            rims = jnp.concatenate([pad_cot[:, :1], pad_cot[:, -1:]], axis=1)
            returned = with_halo(for_sending(rims), (("gx", 1),), 1).astype(rims.dtype)
            cotangent = pad_cot[:, 1:-1]
            cotangent = cotangent.at[:, 0].add(returned[:, 0])
            cotangent = cotangent.at[:, -1].add(returned[:, 3])
        return (cotangent, (jnp.stack(grads_in), jnp.stack(grads_bias), jnp.stack(grads_out)))

    def target_of(position):
        target_slot = lax.dynamic_index_in_dim(batch_order, position, 0, False)
        return lax.dynamic_index_in_dim(targets, target_slot, 0, False)

    clock_ticks = members + section_count - 1

    def forward_tick(clock_tick, carry):
        incoming, saved_inputs, results = carry
        member = clock_tick - section_index
        active = (member >= 0) & (member < members)
        position = jnp.clip(member, 0, members - 1)
        entering = lax.dynamic_index_in_dim(fields, position, 0, False)
        current = jnp.where(section_index == 0, entering, incoming)
        saved_inputs = jnp.where(
            active,
            lax.dynamic_update_index_in_dim(saved_inputs, current, position, 0),
            saved_inputs,
        )
        leaving = run_forward(current, active, local_weights)
        is_last = active & (section_index == section_count - 1)
        results = jnp.where(
            is_last, lax.dynamic_update_index_in_dim(results, leaving, position, 0), results
        )
        incoming = shifted(leaving.astype(jnp.bfloat16), "section", 1).astype(leaving.dtype)
        return (incoming, saved_inputs, results)

    empty_state = jnp.zeros(fields.shape[1:], jnp.float32)
    empty_all = jnp.zeros(fields.shape, jnp.float32)
    _, saved_inputs, results = lax.fori_loop(
        0, clock_ticks, forward_tick, (empty_state, empty_all, empty_all)
    )

    def backward_tick(clock_tick, carry):
        incoming, running = carry
        member = clock_tick - (section_count - 1 - section_index)
        active = (member >= 0) & (member < members)
        position = jnp.clip(member, 0, members - 1)
        current = lax.dynamic_index_in_dim(saved_inputs, position, 0, False)
        result = lax.dynamic_index_in_dim(results, position, 0, False)
        loss_cot = (result - target_of(position)) * loss_scale
        cotangent = jnp.where(section_index == section_count - 1, loss_cot, incoming)
        leaving, grads = run_backward(current, cotangent, active, local_weights)
        running = jax.tree.map(lambda left, right: left + right, running, grads)
        incoming = shifted(for_sending(leaving), "section", -1).astype(leaving.dtype)
        return (incoming, running)

    zero_totals = (
        jnp.zeros(weight_in.shape, jnp.float32),
        jnp.zeros(local_bias.shape, jnp.float32),
        jnp.zeros(weight_out.shape, jnp.float32),
    )
    _, totals = lax.fori_loop(0, clock_ticks, backward_tick, (empty_state, zero_totals))
    summed = lax.psum((totals[0], totals[1], totals[2]), ("gx", "dp"))
    return (summed[0], summed[1], summed[2])


def solution(mesh):
    return jax.shard_map(
        body,
        mesh=mesh,
        in_specs=(
            P("dp", None, "gx", None, None),
            P("dp", None, "gx", None, None),
            P("section", None, None),
            P(),
            P("section", None, None),
            P(),
        ),
        out_specs=(P("section", None, None), P("section", None), P("section", None, None)),
        check_vma=False,
    )
```

profile of v0, /device:TPU:8, one launch (start us, length us, event | category | flops | bytes accessed | tf_op | source)
XLA Modules:
  0.0 603.1 jit_solution(4073102261287004628)
XLA Ops:
  11.2 109.9 %while.49 = (s32[]{:T(128)}, bf16[8,4,8,128]{3,0,2,1:T(8,128)(2,1)S(1)}, bf16[2,8,4,8,128]{4,1,3,2,0:T(8,128)(2,1)S(1)}, f32[2,8,4,8,128]{4,1,3,2,0:T(8,128)S(1)...) while((s32[]{:T(128)}, ...), condition=%wide.region_9.10_spmd.clone, body=%wide.region_0.9_spmd.clone.sunk | while | flops 141885440 | bytes 18625256 | solution.py:202
  11.3 2.7 collective-permute-start
  15.4 4.4 collective-permute-done.1
  21.7 2.0 collective-permute-start.3
  25.4 2.2 collective-permute-done.3
  29.4 2.0 collective-permute-start.5
  33.1 2.2 collective-permute-done.5
  37.1 2.0 collective-permute-start.6
  40.9 4.0 collective-permute-done.7
  52.7 3.4 collective-permute-done.1
  61.6 3.4 collective-permute-done.3
  70.6 3.4 collective-permute-done.5
  79.5 3.4 collective-permute-done.7
  90.7 3.4 collective-permute-done.1
  98.0 3.4 collective-permute-done.3
  103.6 1.8 collective-permute-done.4
  105.4 3.5 collective-permute-done.5
  112.8 3.3 collective-permute-done.7
  116.2 4.0 collective-permute-start.8
  121.1 255.1 %while.50 = (s32[]{:T(128)}, f32[8,4,8,128]{3,0,2,1:T(8,128)S(1)}, f32[4,64,56]{1,2,0:T(8,128)S(1)}, f32[4,64]{1,0:T(4,128)S(1)}, f32[4,8,64]{2,1,0:T(8,128)S(1)...) while((s32[]{:T(128)}, f32[8,4,8,128]{3,0,2,1:T(8,128)S(1)}, ...), condition=%wide.region_29.30_spmd.clone, body=%wide.region_10.29_spmd.clone.sunk | while | flops 506053632 | bytes 81439176 | solution.py:225
  142.0 3.7 collective-permute-done.10
  149.7 3.7 collective-permute-done.12
  155.6 1.8 collective-permute-done.13
  157.5 3.3 collective-permute-done.14
  164.8 3.6 collective-permute-done.16
  172.4 3.4 collective-permute-done.18
  179.7 3.4 collective-permute-done.20
  185.4 1.7 collective-permute-done.21
  187.1 3.4 collective-permute-done.22
  194.5 3.4 collective-permute-done.24
  199.2 11.8 %collective-permute-done.25 = bf16[8,4,8,128]{3,0,2,1:T(8,128)(2,1)S(1)} collective-permute-done((bf16[8,4,8,128]{3,0,2,1:T(8,128)(2,1)S(1)}, bf16[8,4,8,128]{3,0,2,1:T(8,128)(2,1)S(1)}, u32[]{:S(2)}, u32[]{:S(2)}) %collective-permute-start.25) | collective-permute-done | bytes 65568 | tf_op jit(solution)/shard_map/while/body/eval_jaxpr/ppermute | solution.py:37
  214.9 3.5 collective-permute-done.10
  218.5 1.8 conditional.37
  224.2 3.7 collective-permute-done.12
  228.0 1.8 conditional.38
  233.6 3.4 collective-permute-done.14
  237.2 1.8 conditional.39
  242.8 3.5 collective-permute-done.16
  246.5 5.7 conditional.40
  255.9 3.4 collective-permute-done.18
  259.4 3.2 conditional.41
  266.3 3.4 collective-permute-done.20
  269.8 3.2 conditional.42
  276.8 3.4 collective-permute-done.22
  280.2 3.1 conditional.43
  287.2 3.4 collective-permute-done.24
  292.0 1.8 collective-permute-done.25
  297.7 3.4 collective-permute-done.10
  301.2 1.8 conditional.37
  306.9 3.4 collective-permute-done.12
  310.4 1.8 conditional.38
  316.1 3.4 collective-permute-done.14
  319.6 1.8 conditional.39
  325.3 3.4 collective-permute-done.16
  328.8 5.7 conditional.40
  338.3 3.4 collective-permute-done.18
  341.7 3.2 conditional.41
  348.7 3.4 collective-permute-done.20
  352.1 3.2 conditional.42
  359.1 3.4 collective-permute-done.22
  362.5 3.2 conditional.43
  369.6 3.4 collective-permute-done.24
  374.3 1.8 collective-permute-done.25
  376.9 214.9 %all-reduce.11.cloned.1.call-done = (f32[4,64,56]{1,2,0:T(8,128)}, f32[4,64]{1,0:T(4,128)}, f32[4,8,64]{2,1,0:T(8,128)}) async-done(((f32[4,64,56]{1,2,0:T(8,128)}, f32[4,64]{1,0:T(4,128)}, f32[4,8,64]{2,1,0:T(8,128)}), (f32[4,64,56]{1,2,0:T(8,128)}, f32[4,64]{1,0:T(4,128)}, f32[4,8,64]{2,1,0:T(8,128)})) %all-reduce.11.cloned.1.call-update) | async-done | bytes 66576 | tf_op jit(solution)/shard_map/psum | solution.py:226
  (851 shorter events, 205.3 us)
Async XLA Ops:
  7.2 584.6 %all-reduce.11.cloned.1.call-start = ((), (), s32[]{:S(2)}) async-start(), calls=%async_computation | async-start | bytes 266240 | tf_op jit(solution)/shard_map/psum | solution.py:226
  11.3 4.2 collective-permute-start
  14.0 5.8 collective-permute-start.1
  21.6 3.8 collective-permute-start.2
  21.7 5.9 collective-permute-start.3
  29.3 3.8 collective-permute-start.4
  29.4 5.9 collective-permute-start.5
  37.1 3.8 collective-permute-start.6
  39.0 5.8 collective-permute-start.7
  48.8 3.8 collective-permute-start
  50.2 5.8 collective-permute-start.1
  59.2 5.8 collective-permute-start.3
  68.1 5.8 collective-permute-start.5
  75.7 3.8 collective-permute-start.6
  77.1 5.8 collective-permute-start.7
  86.9 3.8 collective-permute-start
  88.3 5.8 collective-permute-start.1
  94.2 3.8 collective-permute-start.2
  95.6 5.8 collective-permute-start.3
  101.5 3.9 collective-permute-start.4
  102.9 6.0 collective-permute-start.5
  109.0 3.8 collective-permute-start.6
  110.3 5.8 collective-permute-start.7
  116.2 4.9 collective-permute-start.8
  138.2 3.8 collective-permute-start.9
  139.8 5.8 collective-permute-start.10
  145.9 3.8 collective-permute-start.11
  147.5 5.8 collective-permute-start.12
  153.5 3.9 collective-permute-start.13
  154.9 5.8 collective-permute-start.14
  160.9 3.8 collective-permute-start.15
  162.5 5.8 collective-permute-start.16
  168.6 3.8 collective-permute-start.17
  169.9 5.8 collective-permute-start.18
  175.9 3.8 collective-permute-start.19
  177.3 5.8 collective-permute-start.20
  183.3 3.8 collective-permute-start.21
  184.6 5.9 collective-permute-start.22
  192.0 5.8 collective-permute-start.24
  197.9 13.1 %collective-permute-start.25 = (bf16[8,4,8,128]{3,0,2,1:T(8,128)(2,1)S(1)}, bf16[8,4,8,128]{3,0,2,1:T(8,128)(2,1)S(1)}, u32[]{:S(2)}, u32[]{:S(2)}) collective-permute-start(bf16[8,4,8,128]{3,0,2,1:T(8,128)(2,1)S(1)} %convert_element_type.895), channel_id=1, source_target_pairs={{128,0},{129,1},{130,2},{131,3},{132,4},{133,5},{134,6},{135,7},{1... | collective-permute-start | bytes 196616 | tf_op jit(solution)/shard_map/while/body/eval_jaxpr/ppermute | solution.py:37
  211.1 3.8 collective-permute-start.9
  212.6 5.8 collective-permute-start.10
  220.4 3.8 collective-permute-start.11
  222.0 5.8 collective-permute-start.12
  229.8 3.8 collective-permute-start.13
  231.2 5.8 collective-permute-start.14
  239.0 3.8 collective-permute-start.15
  240.5 5.8 collective-permute-start.16
  252.1 3.8 collective-permute-start.17
  253.5 5.8 collective-permute-start.18
  262.5 3.8 collective-permute-start.19
  263.9 5.8 collective-permute-start.20
  273.0 3.8 collective-permute-start.21
  274.3 5.8 collective-permute-start.22
  283.4 3.8 collective-permute-start.23
  284.8 5.8 collective-permute-start.24
  295.3 5.8 collective-permute-start.10
  304.5 5.8 collective-permute-start.12
  313.7 5.8 collective-permute-start.14
  322.8 5.8 collective-permute-start.16
  335.8 5.8 collective-permute-start.18
  346.3 5.8 collective-permute-start.20
  356.7 5.8 collective-permute-start.22
  367.1 5.8 collective-permute-start.24
  (20 other events, 168.4 us)
Sparse Core Ops, SparseCore 0:
  377.0 214.7 all-reduce.10
where the time goes:
time: 612 us; the launch traced here: 603 us
  waiting for transfers between devices  417 us (68%)
  starting transfers between devices  86.8 us (14%)
  loops' own time  25.9 us (4%)
  matrix products  25.1 us (4%)
  local copies, waits for them, and re-layouts  20.2 us (3%)
  between operations  14.5 us (2%)
  other arithmetic  13.5 us (2%)
    psum x1, waiting for transfers between devices, body(): summed = lax.psum((totals[0], totals[1], totals[2]), ('gx', 'dp'))  215 us
    ppermute x36, waiting for transfers between devices, with_halo(): before = lax.ppermute(last, axis, up)  123 us
    ppermute x36, waiting for transfers between devices, with_halo(): after = lax.ppermute(initial, axis, down)  61.1 us
    ppermute x36, starting transfers between devices, with_halo(): after = lax.ppermute(initial, axis, down)  50.1 us
    ppermute x36, starting transfers between devices, with_halo(): before = lax.ppermute(last, axis, up)  26.2 us
    ppermute x6, waiting for transfers between devices, shifted(): return lax.ppermute(block, axis, route)  18 us
    another operation x1, loops' own time, body(): lax.fori_loop(0, clock_ticks, backward_tick, (empty_state, zero_totals))  17.9 us
    dot_general x14, matrix products, advance(): jnp.dot(weight_out.astype(jnp.bfloat16), hidden, preferred_element_type=j...  12.3 us
  transfers between devices with their start and end apart: 79, of which 79 were waited for; matrix products, arithmetic and copies ran while one was open for 0% of the time, Pallas kernels for 0%

commit v1 on v0

v1 whole, which is shorter than its diff:
```python
import math

import jax
import jax.numpy as jnp
from jax import lax
from jax.experimental import pallas as pl
from jax.experimental.pallas import tpu as pltpu
from jax.sharding import PartitionSpec as P

CORRECTION_GAIN = 0.1
LOSS_GAIN = 8.0
SPEED_X = 0.2
DIFFUSE_X = 0.25
SPEED_Y = 0.15
SPEED_Z = 0.1
KEEP = 1.0 - SPEED_X - 2.0 * DIFFUSE_X - SPEED_Y - SPEED_Z

F32 = jnp.float32
BF16 = jnp.bfloat16

STEPS = 8
C = 8
H = 64
FEATS = 64
LANES = 128
NX = 64
NY = 8
NZ = 128
ROW = NX * NY
TILES = ROW // LANES
SLABS = 16
OWN = NZ // SLABS
WIN = 40
OWN_AT = 16
TWIN = 24
CHUNK = WIN + TWIN
SLAB_CELLS = 32
PAD = 4
VMEM_LIMIT = 56 * 1024 * 1024


def prepare_kernel(slots, fields, targets, out):
    field = fields[slots[0]].T
    target = targets[slots[1]].T
    field = jnp.concatenate([field[NZ - OWN_AT :], field, field[: WIN - OWN_AT]], axis=0)
    target = jnp.concatenate([target[NZ - OWN :], target, target[: TWIN - OWN]], axis=0)
    for slab in range(SLABS):
        begin = slab * OWN
        both = jnp.concatenate(
            [field[begin : begin + WIN], target[begin : begin + TWIN]], axis=0
        )
        out[slab] = both.astype(BF16)


def roll_lanes(tile, shift):
    return pltpu.roll(tile, shift % LANES, 1)


def split(row):
    return [row[:, LANES * t : LANES * (t + 1)] for t in range(TILES)]


def join(tiles):
    return jnp.concatenate(tiles, axis=1)


class Shifts:
    def __init__(self):
        lane = lax.broadcasted_iota(jnp.int32, (C, LANES), 1)
        self.first_x = lane < NY
        self.last_x = lane >= LANES - NY
        self.first_y = lane % NY == 0
        self.last_y = lane % NY == NY - 1

    def x_from_below(self, row):
        rolled = [roll_lanes(t, NY) for t in split(row)]
        return join(
            [jnp.where(self.first_x, rolled[t - 1], rolled[t]) for t in range(TILES)]
        )

    def x_from_above(self, row):
        rolled = [roll_lanes(t, -NY) for t in split(row)]
        return join(
            [
                jnp.where(self.last_x, rolled[(t + 1) % TILES], rolled[t])
                for t in range(TILES)
            ]
        )

    def y_from_below(self, row):
        return join(
            [
                jnp.where(self.first_y, roll_lanes(t, 1 - NY), roll_lanes(t, 1))
                for t in split(row)
            ]
        )

    def y_from_above(self, row):
        return join(
            [
                jnp.where(self.last_y, roll_lanes(t, NY - 1), roll_lanes(t, -1))
                for t in split(row)
            ]
        )


def neighbours(shifts, rows):
    blocks = []
    for below, row, above in zip(rows[:-2], rows[1:-1], rows[2:]):
        blocks.append(
            (
                row,
                shifts.x_from_below(row),
                shifts.x_from_above(row),
                shifts.y_from_below(row),
                shifts.y_from_above(row),
                below,
                above,
            )
        )
    return blocks


def feature_matrix(blocks):
    ones = jnp.ones((C, ROW), F32)
    return join([jnp.concatenate(b + (ones,), axis=0).astype(BF16) for b in blocks])


def rollout_kernel(received, weights, out, fields, target, acts, unpack, c0, c5, c6):
    shifts = Shifts()
    lane = lax.broadcasted_iota(jnp.int32, (16, LANES), 1) // SLAB_CELLS
    low_bit = lane % 2 == 0
    high_bit = lane < 2

    for quarter in range(CHUNK // 16):
        for half in range(2):
            for tile in range(TILES):
                v = [
                    received[
                        4 * tile + a,
                        pl.ds(16 * quarter, 16),
                        pl.ds(LANES * half, LANES),
                    ].astype(F32)
                    for a in range(4)
                ]
                t = [None] * 4
                for a in (0, 2):
                    t[a] = jnp.where(low_bit, v[a], roll_lanes(v[a + 1], SLAB_CELLS))
                    t[a + 1] = jnp.where(low_bit, roll_lanes(v[a], -SLAB_CELLS), v[a + 1])
                o = [None] * 4
                for b in (0, 1):
                    o[b] = jnp.where(high_bit, t[b], roll_lanes(t[b + 2], 2 * SLAB_CELLS))
                    o[b + 2] = jnp.where(
                        high_bit, roll_lanes(t[b], -2 * SLAB_CELLS), t[b + 2]
                    )
                for b in range(4):
                    unpack[tile, pl.ds((4 * half + b) * CHUNK + 16 * quarter, 16), :] = o[b]

    def plane(at):
        return join([unpack[t, pl.ds(at, C, stride=CHUNK), :] for t in range(TILES)])

    for w in range(WIN):
        fields[0, PAD + w] = plane(w)
    for w in range(TWIN):
        target[w] = plane(WIN + w)

    def forward_rows(step, begin, count):
        rows = [fields[step, PAD + begin + i - 1] for i in range(count + 2)]
        blocks = neighbours(shifts, rows)
        stacked = feature_matrix(blocks)
        w_in = weights[step, :H, :].astype(BF16)
        w_out = weights[step, H : H + C, :].astype(BF16)
        act = jnp.tanh(jnp.dot(w_in, stacked, preferred_element_type=F32))
        correction = jnp.dot(w_out, act.astype(BF16), preferred_element_type=F32)
        after = []
        for i, (u, xm, xp, ym, _, zm, _) in enumerate(blocks):
            after.append(
                KEEP * u
                + (SPEED_X + DIFFUSE_X) * xm
                + DIFFUSE_X * xp
                + SPEED_Y * ym
                + SPEED_Z * zm
                + CORRECTION_GAIN * correction[:, ROW * i : ROW * (i + 1)]
            )
        return act, after

    def forward_step(step, _):
        def inner(block, _):
            begin = OWN_AT - OWN + block * OWN
            act, after = forward_rows(step, begin, OWN)
            for i in range(OWN):
                acts[step, begin - (OWN_AT - OWN) + i] = act[:, ROW * i : ROW * (i + 1)]
            for i in range(OWN):
                fields[step + 1, PAD + begin + i] = after[i]
            return 0

        lax.fori_loop(0, 3, inner, 0)

        def outer(block, _):
            low = OWN_AT - OWN - 3 * (block + 1)
            high = OWN_AT + 2 * OWN + 3 * block
            _, after_low = forward_rows(step, low, 3)
            _, after_high = forward_rows(step, high, 3)
            for i in range(3):
                fields[step + 1, PAD + low + i] = after_low[i]
                fields[step + 1, PAD + high + i] = after_high[i]
            return 0

        lax.fori_loop(0, (6 - jnp.minimum(step, 6) + 2) // 3, outer, 0)
        return 0

    lax.fori_loop(0, STEPS, forward_step, 0)

    loss_scale = LOSS_GAIN / math.sqrt(16 * C * NX * NY * NZ)
    first = STEPS % 2
    c5[...] = jnp.zeros(c5.shape, F32)
    c6[...] = jnp.zeros(c6.shape, F32)
    c0[...] = jnp.zeros(c0.shape, F32)
    for w in range(TWIN):
        c0[STEPS % 2, PAD + w] = (
            fields[STEPS, PAD + OWN_AT - OWN + w] - target[w]
        ) * loss_scale

    def backward_rows(step, begin, count, own):
        now = (step + 1) % 2
        cots = []
        for i in range(count):
            at = PAD + begin + i
            cots.append(c0[now, at] + c5[now, at + 1] + c6[now, at - 1])
        act = join([acts[step, begin + i] for i in range(count)])
        w_in = weights[step, :H, :].T[: 7 * C].astype(BF16)
        w_out = weights[step, H : H + 2 * C, :].T.astype(BF16)
        cot_corr = (CORRECTION_GAIN * join(cots)).astype(BF16)
        cot_wide = jnp.concatenate([cot_corr, jnp.zeros_like(cot_corr)], axis=0)
        cot_pre = jnp.dot(w_out, cot_wide, preferred_element_type=F32) * (1.0 - act * act)
        cot_half = cot_pre.astype(BF16)
        cot_stack = jnp.dot(w_in, cot_half, preferred_element_type=F32)
        grad = None
        if own:
            rows = [
                fields[step, PAD + OWN_AT - OWN + begin + i - 1] for i in range(count + 2)
            ]
            stacked = feature_matrix(neighbours(shifts, rows))
            left = jnp.concatenate([cot_half, cot_wide], axis=0)
            right = jnp.concatenate([stacked, act.astype(BF16)], axis=0)
            grad = lax.dot_general(
                left, right, (((1,), (1,)), ((), ())), preferred_element_type=F32
            )
        new = []
        for i in range(count):
            cot = cots[i]
            parts = [
                cot_stack[C * b : C * (b + 1), ROW * i : ROW * (i + 1)] for b in range(7)
            ]
            centre = (
                KEEP * cot
                + parts[0]
                + shifts.x_from_above(parts[1] + (SPEED_X + DIFFUSE_X) * cot)
                + shifts.x_from_below(parts[2] + DIFFUSE_X * cot)
                + shifts.y_from_above(parts[3] + SPEED_Y * cot)
                + shifts.y_from_below(parts[4])
            )
            new.append((centre, parts[5] + SPEED_Z * cot, parts[6]))
        return new, grad

    def store(step, begin, new):
        then = step % 2
        for i, (centre, minus, plus) in enumerate(new):
            at = PAD + begin + i
            c0[then, at] = centre
            c5[then, at] = minus
            c6[then, at] = plus

    half = lax.broadcasted_iota(jnp.int32, (H + C, LANES), 1) < FEATS

    def backward_step(back, _):
        step = STEPS - 1 - back
        new, grad = backward_rows(step, OWN, OWN, True)
        store(step, OWN, new)
        mixed = jnp.concatenate(
            [grad[:H], pltpu.roll(grad[H : H + C], FEATS, 1)], axis=0
        )
        turned = pltpu.roll(mixed, FEATS, 1)
        odd = step % 2 == 1

        @pl.when(odd)
        def _():
            out[step // 2] = jnp.where(half, 0.0, turned)

        @pl.when(jnp.logical_not(odd))
        def _():
            out[step // 2] = jnp.where(half, mixed, out[step // 2])

        def ghosts(block, _):
            low = OWN - 4 * (block + 1)
            high = 2 * OWN + 4 * block
            new_low, _ = backward_rows(step, low, 4, False)
            new_high, _ = backward_rows(step, high, 4, False)
            store(step, low, new_low)
            store(step, high, new_high)
            return 0

        lax.fori_loop(0, (step + 3) // 4, ghosts, 0)
        return 0

    lax.fori_loop(0, STEPS, backward_step, 0)


def vmem():
    return pl.BlockSpec(memory_space=pltpu.VMEM)


def prepare(slots, fields, targets):
    return pl.pallas_call(
        prepare_kernel,
        out_shape=jax.ShapeDtypeStruct((SLABS, CHUNK, C * SLAB_CELLS), BF16),
        in_specs=[pl.BlockSpec(memory_space=pltpu.SMEM), vmem(), vmem()],
        out_specs=vmem(),
        compiler_params=pltpu.CompilerParams(vmem_limit_bytes=VMEM_LIMIT),
        name="prepare",
    )(slots, fields, targets)


def rollout(received, weights):
    return pl.pallas_call(
        rollout_kernel,
        out_shape=jax.ShapeDtypeStruct((STEPS // 2, H + C, LANES), F32),
        in_specs=[vmem(), vmem()],
        out_specs=vmem(),
        scratch_shapes=[
            pltpu.VMEM((STEPS + 1, WIN + 2 * PAD, C, ROW), F32),
            pltpu.VMEM((TWIN, C, ROW), F32),
            pltpu.VMEM((STEPS, TWIN, H, ROW), F32),
            pltpu.VMEM((TILES, C * CHUNK, LANES), F32),
            pltpu.VMEM((2, TWIN + 2 * PAD, C, ROW), F32),
            pltpu.VMEM((2, TWIN + 2 * PAD, C, ROW), F32),
            pltpu.VMEM((2, TWIN + 2 * PAD, C, ROW), F32),
        ],
        compiler_params=pltpu.CompilerParams(vmem_limit_bytes=VMEM_LIMIT),
        name="rollout",
    )(received, weights)


def swap(block, axis, distance):
    devices = lax.axis_size(axis)
    return lax.ppermute(block, axis, [(i, i ^ distance) for i in range(devices)])


def exchange_sum(block, axis, distances):
    arrived = [swap(block, axis, d) for d in distances]
    for other in arrived:
        block = block + other
    return block


def all_weights(weight_in, bias_in, weight_out, section):
    depth = weight_in.shape[0]
    packed = jnp.concatenate(
        [jnp.pad(weight_in, ((0, 0), (0, 0), (0, FEATS - 7 * C))), weight_out], axis=1
    ).astype(BF16)
    other = swap(packed, "section", 1)
    mine, other = packed.astype(F32), other.astype(F32)
    first = section == 0
    whole = jnp.concatenate(
        [jnp.where(first, mine, other), jnp.where(first, other, mine)], axis=0
    )
    high = lax.reduce_precision(bias_in, 8, 7)
    middle = lax.reduce_precision(bias_in - high, 8, 7)
    low = bias_in - high - middle
    columns = jnp.stack([high, middle, low], axis=2)
    columns = jnp.pad(columns, ((0, 0), (0, C), (7 * C, FEATS - 7 * C - 3)))
    return jnp.pad(whole + columns, ((0, 0), (0, C), (0, 0)))


def body(fields, targets, weight_in, bias_in, weight_out, batch_order):
    section = lax.axis_index("section")
    members = fields.shape[0]
    depth = weight_in.shape[0]
    slots = jnp.stack([section, batch_order[section]]).astype(jnp.int32)
    flat = (members, C * SLAB_CELLS, NZ)
    windows = prepare(slots, fields.reshape(flat), targets.reshape(flat))
    weights = all_weights(weight_in, bias_in, weight_out, section)
    received = lax.all_to_all(windows, "gx", 0, 0, tiled=True)
    grads = rollout(received, weights)
    pairs = depth // 2
    mine = lax.dynamic_slice_in_dim(grads, section * pairs, pairs, 0)
    yours = lax.dynamic_slice_in_dim(grads, (1 - section) * pairs, pairs, 0)
    total = mine + swap(yours, "section", 1)
    total = exchange_sum(total, "gx", (1, 2, 3))
    total = exchange_sum(total, "gx", (4, 8, 12))
    for distance in (1, 2, 4):
        total = exchange_sum(total, "dp", (distance,))
    total = total.reshape(pairs, H + C, 2, FEATS).transpose(0, 2, 1, 3)
    total = total.reshape(depth, H + C, FEATS)
    return (total[:, :H, : 7 * C], total[:, :H, 7 * C], total[:, H:, :])


def solution(mesh):
    return jax.shard_map(
        body,
        mesh=mesh,
        in_specs=(
            P("dp", None, "gx", None, None),
            P("dp", None, "gx", None, None),
            P("section", None, None),
            P(),
            P("section", None, None),
            P(),
        ),
        out_specs=(P("section", None, None), P("section", None), P("section", None, None)),
        check_vma=False,
    )
```

time: 612 us -> 103 us (0.17); the launches traced: 603 us -> 103 us
  waiting for transfers between devices: 417 us -> 23.1 us
  starting transfers between devices: 86.8 us -> 30.1 us
  Pallas kernels: 0 us -> 40 us
  loops' own time: 25.9 us -> 0 us
  matrix products: 25.1 us -> 0 us
  between operations: 14.5 us -> 0.75 us
  local copies, waits for them, and re-layouts: 20.2 us -> 7.36 us
  other arithmetic: 13.5 us -> 1.54 us
    psum x1 -> x0, waiting for transfers between devices: 215 us -> none  [body(): summed = lax.psum((totals[0], totals[1], totals[2]), ('gx', 'dp'))]
    ppermute x78 -> x11, waiting for transfers between devices: 202 us -> 17.2 us  [swap(): lax.ppermute(block, axis, [(i, i ^ distance) for i in range(devices)])]
    ppermute x78 -> x11, starting transfers between devices: 86.8 us -> 22.6 us  [swap(): lax.ppermute(block, axis, [(i, i ^ distance) for i in range(devices)])]
    pallas_call x0 -> x2, Pallas kernels: none -> 40 us  [the longest x1 38.1 us: rollout(): pl.pallas_call(rollout_kernel, out_shape=jax.ShapeDtypeStruct((STEPS // 2...]
    another operation x35 -> x0, loops' own time: 25.9 us -> none  [the longest x1 17.9 us: body(): lax.fori_loop(0, clock_ticks, backward_tick, (empty_state, zero_totals))]
    dot_general x54 -> x0, matrix products: 25.1 us -> none  [the longest x14 12.3 us: advance(): jnp.dot(weight_out.astype(jnp.bfloat16), hidden, preferred_element_type=j...]
    all_to_all x0 -> x1, starting transfers between devices: none -> 7.52 us  [body(): received = lax.all_to_all(windows, 'gx', 0, 0, tiled=True)]
  transfers between devices with their start and end apart: 79 -> 12, of which waited for: 79 -> 11; matrix products, arithmetic and copies ran while one was open for 0% -> 1% of each run, Pallas kernels for 0% -> 0%
where the time goes in v1:
time: 103 us
  Pallas kernels  40 us (39%)
  starting transfers between devices  30.1 us (29%)
  waiting for transfers between devices  23.1 us (22%)
  local copies, waits for them, and re-layouts  7.36 us (7%)
  other arithmetic  1.54 us (1%)
    pallas_call x1, Pallas kernels, rollout(): pl.pallas_call(rollout_kernel, out_shape=jax.ShapeDtypeStruct((STEPS // 2...  38.1 us
    ppermute x11, starting transfers between devices, swap(): lax.ppermute(block, axis, [(i, i ^ distance) for i in range(devices)])  22.6 us
    ppermute x11, waiting for transfers between devices, swap(): lax.ppermute(block, axis, [(i, i ^ distance) for i in range(devices)])  17.2 us
    all_to_all x1, starting transfers between devices, body(): received = lax.all_to_all(windows, 'gx', 0, 0, tiled=True)  7.52 us
    all_to_all x1, waiting for transfers between devices, body(): received = lax.all_to_all(windows, 'gx', 0, 0, tiled=True)  5.92 us
    unnamed x13, local copies, waits for them, and re-layouts  3.37 us
  transfers between devices with their start and end apart: 12, of which 11 were waited for; matrix products, arithmetic and copies ran while one was open for 1% of the time, Pallas kernels for 0%

profile of v1, /device:TPU:8, one launch (start us, length us, event | category | flops | bytes accessed | tf_op | source)
XLA Modules:
  0.0 102.9 jit_solution(16918474931902767691)
XLA Ops:
  0.6 0.0 copy-start.5
  0.6 0.6 copy-done.5
  1.3 0.6 dynamic_slice.9
  1.9 1.2 %pad_add_fusion.slots = s32[2]{0:T(128)} fusion(s32[1]{0:T(128)} %dynamic_slice.9, s32[1]{0:T(128)} %bitcast), kind=kLoop, calls=%fused_computation.17 | loop fusion | flops 2 | bytes 16 | tf_op jit(solution)/shard_map/stack | solution.py:379
  3.1 1.9 %prepare.1 = bf16[16,64,256]{2,1,0:T(8,128)(2,1)} custom-call(s32[2]{0:T(128)} %pad_add_fusion.slots, f32[2,256,128]{2,1,0:T(8,128)} %bitcast.13, f32[2,256,128]{2,1,0:T(8,128)} %bitcast.14), custom_call_target="tpu_custom_call" | custom-call | tf_op jit(solution)/shard_map/prepare/pallas_call | solution.py:314
  5.0 0.0 copy-start.2
  5.1 7.5 %all-to-all-start = ((bf16[16,64,256]{2,1,0:T(8,128)(2,1)}), bf16[16,64,256]{2,1,0:T(8,128)(2,1)S(1)}, u32[]{:S(2)}, u32[]{:S(2)}) async-start(bf16[16,64,256]{2,1,0:T(8,128)(2,1)} %prepare.1), calls=%async_computation | async-start | bytes 1048576 | tf_op jit(solution)/shard_map/all_to_all | solution.py:383
  12.6 0.0 copy-done.2
  12.6 0.0 copy-start.3
  12.6 0.1 copy.29
  12.7 0.6 copy-done.3
  13.3 0.0 copy-start.4
  13.3 0.1 collective-permute-start
  13.5 0.6 copy-done.4
  14.0 0.1 copy.30
  14.2 0.5 collective-permute-done
  14.7 0.1 maximum_add_fusion
  14.9 0.7 pad.15.weights
  15.6 5.9 %all-to-all-done.received = bf16[16,64,256]{2,1,0:T(8,128)(2,1)S(1)} async-done(((bf16[16,64,256]{2,1,0:T(8,128)(2,1)}), bf16[16,64,256]{2,1,0:T(8,128)(2,1)S(1)}, u32[]{:S(2)}, u32[]{:S(2)}) %all-to-all-start) | async-done | bytes 524320 | tf_op jit(solution)/shard_map/all_to_all | solution.py:383
  21.5 0.0 copy-start
  21.5 0.8 copy-done
  22.3 38.1 %rollout.1 = f32[4,72,128]{2,1,0:T(8,128)} custom-call(bf16[16,64,256]{2,1,0:T(8,128)(2,1)} %copy-done, f32[8,80,64]{2,1,0:T(8,128)} %pad.15.weights), custom_call_target="tpu_custom_call" | custom-call | tf_op jit(solution)/shard_map/rollout/pallas_call | solution.py:325
  60.4 0.0 copy-start.1
  60.4 1.0 constant_dynamic-slice_fusion
  61.4 0.0 collective-permute-start.1
  61.4 1.3 %collective-permute-done.1 = f32[2,72,128]{2,1,0:T(8,128)S(1)} collective-permute-done((f32[2,72,128]{2,1,0:T(8,128)S(1)}, f32[2,72,128]{2,1,0:T(8,128)S(1)}, u32[]{:S(2)}, u32[]{:S(2)}) %collective-permute-start.1) | collective-permute-done | bytes 73760 | tf_op jit(solution)/shard_map/ppermute | solution.py:346
  62.7 0.0 copy-done.1
  62.7 1.8 %collective-permute-start.4 = (f32[2,72,128]{2,1,0:T(8,128)S(1)}, f32[2,72,128]{2,1,0:T(8,128)S(1)}, u32[]{:S(2)}, u32[]{:S(2)}) collective-permute-start(f32[2,72,128]{2,1,0:T(8,128)S(1)} %dynamic-slice_add_fusion), channel_id=1, source_target_pairs={{0,24},{8,16},{16,8},{24,0},{32,56},{40,48},{48,40},{56,32},{64,88... | collective-permute-start | bytes 221192 | tf_op jit(solution)/shard_map/ppermute | solution.py:346
  64.5 1.1 %collective-permute-start.3 = (f32[2,72,128]{2,1,0:T(8,128)S(1)}, f32[2,72,128]{2,1,0:T(8,128)S(1)}, u32[]{:S(2)}, u32[]{:S(2)}) collective-permute-start(f32[2,72,128]{2,1,0:T(8,128)S(1)} %dynamic-slice_add_fusion), channel_id=1, source_target_pairs={{0,16},{8,24},{16,0},{24,8},{32,48},{40,56},{48,32},{56,40},{64,80... | collective-permute-start | bytes 221192 | tf_op jit(solution)/shard_map/ppermute | solution.py:346
  65.6 1.3 %collective-permute-start.2 = (f32[2,72,128]{2,1,0:T(8,128)S(1)}, f32[2,72,128]{2,1,0:T(8,128)S(1)}, u32[]{:S(2)}, u32[]{:S(2)}) collective-permute-start(f32[2,72,128]{2,1,0:T(8,128)S(1)} %dynamic-slice_add_fusion), channel_id=1, source_target_pairs={{0,8},{8,0},{16,24},{24,16},{32,40},{40,32},{48,56},{56,48},{64,72... | collective-permute-start | bytes 221192 | tf_op jit(solution)/shard_map/ppermute | solution.py:346
  66.9 1.5 %collective-permute-done.4 = f32[2,72,128]{2,1,0:T(8,128)S(1)} collective-permute-done((f32[2,72,128]{2,1,0:T(8,128)S(1)}, f32[2,72,128]{2,1,0:T(8,128)S(1)}, u32[]{:S(2)}, u32[]{:S(2)}) %collective-permute-start.4) | collective-permute-done | bytes 73760 | tf_op jit(solution)/shard_map/ppermute | solution.py:346
  68.3 2.5 %collective-permute-done.3 = f32[2,72,128]{2,1,0:T(8,128)S(1)} collective-permute-done((f32[2,72,128]{2,1,0:T(8,128)S(1)}, f32[2,72,128]{2,1,0:T(8,128)S(1)}, u32[]{:S(2)}, u32[]{:S(2)}) %collective-permute-start.3) | collective-permute-done | bytes 73760 | tf_op jit(solution)/shard_map/ppermute | solution.py:346
  70.8 0.0 collective-permute-done.2
  70.9 1.2 %collective-permute-start.7 = (f32[2,72,128]{2,1,0:T(8,128)S(1)}, f32[2,72,128]{2,1,0:T(8,128)S(1)}, u32[]{:S(2)}, u32[]{:S(2)}) collective-permute-start(f32[2,72,128]{2,1,0:T(8,128)S(1)} %add_add_fusion.1), channel_id=1, source_target_pairs={{0,96},{8,104},{16,112},{24,120},{32,64},{40,72},{48,80},{56,88},{... | collective-permute-start | bytes 221192 | tf_op jit(solution)/shard_map/ppermute | solution.py:346
  72.0 3.3 %collective-permute-start.6 = (f32[2,72,128]{2,1,0:T(8,128)S(1)}, f32[2,72,128]{2,1,0:T(8,128)S(1)}, u32[]{:S(2)}, u32[]{:S(2)}) collective-permute-start(f32[2,72,128]{2,1,0:T(8,128)S(1)} %add_add_fusion.1), channel_id=1, source_target_pairs={{0,64},{8,72},{16,80},{24,88},{32,96},{40,104},{48,112},{56,120},{... | collective-permute-start | bytes 221192 | tf_op jit(solution)/shard_map/ppermute | solution.py:346
  75.3 0.0 collective-permute-start.5
  75.3 0.8 collective-permute-done.7
  76.1 1.8 %collective-permute-done.6 = f32[2,72,128]{2,1,0:T(8,128)S(1)} collective-permute-done((f32[2,72,128]{2,1,0:T(8,128)S(1)}, f32[2,72,128]{2,1,0:T(8,128)S(1)}, u32[]{:S(2)}, u32[]{:S(2)}) %collective-permute-start.6) | collective-permute-done | bytes 73760 | tf_op jit(solution)/shard_map/ppermute | solution.py:346
  77.9 1.8 %collective-permute-done.5 = f32[2,72,128]{2,1,0:T(8,128)S(1)} collective-permute-done((f32[2,72,128]{2,1,0:T(8,128)S(1)}, f32[2,72,128]{2,1,0:T(8,128)S(1)}, u32[]{:S(2)}, u32[]{:S(2)}) %collective-permute-start.5) | collective-permute-done | bytes 73760 | tf_op jit(solution)/shard_map/ppermute | solution.py:346
  79.7 2.0 %collective-permute-start.8 = (f32[2,72,128]{2,1,0:T(8,128)S(1)}, f32[2,72,128]{2,1,0:T(8,128)S(1)}, u32[]{:S(2)}, u32[]{:S(2)}) collective-permute-start(f32[2,72,128]{2,1,0:T(8,128)S(1)} %add_add_fusion), channel_id=1, source_target_pairs={{0,1},{1,0},{2,3},{3,2},{4,5},{5,4},{6,7},{7,6},{8,9},{9,8},{10,11... | collective-permute-start | bytes 221192 | tf_op jit(solution)/shard_map/ppermute | solution.py:346
  81.7 2.4 %collective-permute-done.8 = f32[2,72,128]{2,1,0:T(8,128)S(1)} collective-permute-done((f32[2,72,128]{2,1,0:T(8,128)S(1)}, f32[2,72,128]{2,1,0:T(8,128)S(1)}, u32[]{:S(2)}, u32[]{:S(2)}) %collective-permute-start.8) | collective-permute-done | bytes 73760 | tf_op jit(solution)/shard_map/ppermute | solution.py:346
  84.1 3.6 %collective-permute-start.9 = (f32[2,72,128]{2,1,0:T(8,128)S(1)}, f32[2,72,128]{2,1,0:T(8,128)S(1)}, u32[]{:S(2)}, u32[]{:S(2)}) collective-permute-start(f32[2,72,128]{2,1,0:T(8,128)S(1)} %add.59), channel_id=1, source_target_pairs={{0,2},{1,3},{2,0},{3,1},{4,6},{5,7},{6,4},{7,5},{8,10},{9,11},{10,... | collective-permute-start | bytes 221192 | tf_op jit(solution)/shard_map/ppermute | solution.py:346
  87.7 2.3 %collective-permute-done.9 = f32[2,72,128]{2,1,0:T(8,128)S(1)} collective-permute-done((f32[2,72,128]{2,1,0:T(8,128)S(1)}, f32[2,72,128]{2,1,0:T(8,128)S(1)}, u32[]{:S(2)}, u32[]{:S(2)}) %collective-permute-start.9) | collective-permute-done | bytes 73760 | tf_op jit(solution)/shard_map/ppermute | solution.py:346
  90.1 8.3 %collective-permute-start.10 = (f32[2,72,128]{2,1,0:T(8,128)S(1)}, f32[2,72,128]{2,1,0:T(8,128)S(1)}, u32[]{:S(2)}, u32[]{:S(2)}) collective-permute-start(f32[2,72,128]{2,1,0:T(8,128)S(1)} %add.60), channel_id=1, source_target_pairs={{0,4},{1,5},{2,6},{3,7},{4,0},{5,1},{6,2},{7,3},{8,12},{9,13},{10,... | collective-permute-start | bytes 221192 | tf_op jit(solution)/shard_map/ppermute | solution.py:346
  98.4 2.3 %collective-permute-done.10 = f32[2,72,128]{2,1,0:T(8,128)S(1)} collective-permute-done((f32[2,72,128]{2,1,0:T(8,128)S(1)}, f32[2,72,128]{2,1,0:T(8,128)S(1)}, u32[]{:S(2)}, u32[]{:S(2)}) %collective-permute-start.10) | collective-permute-done | bytes 73760 | tf_op jit(solution)/shard_map/ppermute | solution.py:346
  100.7 0.1 fusion.3
  100.8 0.8 slice_reduce_fusion
  101.6 0.6 slice.24
  102.2 0.7 copy.31
  (14 shorter events, 0.2 us)
Async XLA Ops:
  0.6 0.7 copy-start.5
  5.0 7.5 %copy-start.2 = (f32[4,64,56]{1,2,0:T(8,128)S(1)}, f32[4,64,56]{1,2,0:T(8,128)}, u32[]{:S(2)}) copy-start(f32[4,64,56]{1,2,0:T(8,128)} %param.8) | copy-start | bytes 172036
  5.1 16.5 %all-to-all-start = ((bf16[16,64,256]{2,1,0:T(8,128)(2,1)}), bf16[16,64,256]{2,1,0:T(8,128)(2,1)S(1)}, u32[]{:S(2)}, u32[]{:S(2)}) async-start(bf16[16,64,256]{2,1,0:T(8,128)(2,1)} %prepare.1), calls=%async_computation | async-start | bytes 1048576 | tf_op jit(solution)/shard_map/all_to_all | solution.py:383
  12.6 0.7 copy-start.3
  13.3 0.7 copy-start.4
  13.3 1.4 %collective-permute-start = (bf16[4,72,64]{2,1,0:T(8,128)(2,1)S(1)}, bf16[4,72,64]{2,1,0:T(8,128)(2,1)S(1)}, u32[]{:S(2)}, u32[]{:S(2)}) collective-permute-start(bf16[4,72,64]{2,1,0:T(8,128)(2,1)S(1)} %fusion.1), channel_id=1, source_target_pairs={{0,128},{128,0},{1,129},{129,1},{2,130},{130,2},{3,131},{131,3},{4... | collective-permute-start | bytes 110600 | tf_op jit(solution)/shard_map/ppermute | solution.py:346
  21.5 0.8 copy-start
  60.4 2.2 %copy-start.1 = (f32[4,72,128]{2,1,0:T(8,128)S(1)}, f32[4,72,128]{2,1,0:T(8,128)}, u32[]{:S(2)}) copy-start(f32[4,72,128]{2,1,0:T(8,128)} %rollout.1) | copy-start | bytes 442372
  61.4 1.3 %collective-permute-start.1 = (f32[2,72,128]{2,1,0:T(8,128)S(1)}, f32[2,72,128]{2,1,0:T(8,128)S(1)}, u32[]{:S(2)}, u32[]{:S(2)}) collective-permute-start(f32[2,72,128]{2,1,0:T(8,128)S(1)} %constant_dynamic-slice_fusion), channel_id=1, source_target_pairs={{0,128},{128,0},{1,129},{129,1},{2,130},{130,2},{3,131},{131,3},{4... | collective-permute-start | bytes 221192 | tf_op jit(solution)/shard_map/ppermute | solution.py:346
  62.7 5.7 %collective-permute-start.4 = (f32[2,72,128]{2,1,0:T(8,128)S(1)}, f32[2,72,128]{2,1,0:T(8,128)S(1)}, u32[]{:S(2)}, u32[]{:S(2)}) collective-permute-start(f32[2,72,128]{2,1,0:T(8,128)S(1)} %dynamic-slice_add_fusion), channel_id=1, source_target_pairs={{0,24},{8,16},{16,8},{24,0},{32,56},{40,48},{48,40},{56,32},{64,88... | collective-permute-start | bytes 221192 | tf_op jit(solution)/shard_map/ppermute | solution.py:346
  64.5 6.3 %collective-permute-start.3 = (f32[2,72,128]{2,1,0:T(8,128)S(1)}, f32[2,72,128]{2,1,0:T(8,128)S(1)}, u32[]{:S(2)}, u32[]{:S(2)}) collective-permute-start(f32[2,72,128]{2,1,0:T(8,128)S(1)} %dynamic-slice_add_fusion), channel_id=1, source_target_pairs={{0,16},{8,24},{16,0},{24,8},{32,48},{40,56},{48,32},{56,40},{64,80... | collective-permute-start | bytes 221192 | tf_op jit(solution)/shard_map/ppermute | solution.py:346
  65.6 5.3 %collective-permute-start.2 = (f32[2,72,128]{2,1,0:T(8,128)S(1)}, f32[2,72,128]{2,1,0:T(8,128)S(1)}, u32[]{:S(2)}, u32[]{:S(2)}) collective-permute-start(f32[2,72,128]{2,1,0:T(8,128)S(1)} %dynamic-slice_add_fusion), channel_id=1, source_target_pairs={{0,8},{8,0},{16,24},{24,16},{32,40},{40,32},{48,56},{56,48},{64,72... | collective-permute-start | bytes 221192 | tf_op jit(solution)/shard_map/ppermute | solution.py:346
  70.9 5.2 %collective-permute-start.7 = (f32[2,72,128]{2,1,0:T(8,128)S(1)}, f32[2,72,128]{2,1,0:T(8,128)S(1)}, u32[]{:S(2)}, u32[]{:S(2)}) collective-permute-start(f32[2,72,128]{2,1,0:T(8,128)S(1)} %add_add_fusion.1), channel_id=1, source_target_pairs={{0,96},{8,104},{16,112},{24,120},{32,64},{40,72},{48,80},{56,88},{... | collective-permute-start | bytes 221192 | tf_op jit(solution)/shard_map/ppermute | solution.py:346
  72.0 5.9 %collective-permute-start.6 = (f32[2,72,128]{2,1,0:T(8,128)S(1)}, f32[2,72,128]{2,1,0:T(8,128)S(1)}, u32[]{:S(2)}, u32[]{:S(2)}) collective-permute-start(f32[2,72,128]{2,1,0:T(8,128)S(1)} %add_add_fusion.1), channel_id=1, source_target_pairs={{0,64},{8,72},{16,80},{24,88},{32,96},{40,104},{48,112},{56,120},{... | collective-permute-start | bytes 221192 | tf_op jit(solution)/shard_map/ppermute | solution.py:346
  75.3 4.4 %collective-permute-start.5 = (f32[2,72,128]{2,1,0:T(8,128)S(1)}, f32[2,72,128]{2,1,0:T(8,128)S(1)}, u32[]{:S(2)}, u32[]{:S(2)}) collective-permute-start(f32[2,72,128]{2,1,0:T(8,128)S(1)} %add_add_fusion.1), channel_id=1, source_target_pairs={{0,32},{8,40},{16,48},{24,56},{32,0},{40,8},{48,16},{56,24},{64,96... | collective-permute-start | bytes 221192 | tf_op jit(solution)/shard_map/ppermute | solution.py:346
  79.7 4.4 %collective-permute-start.8 = (f32[2,72,128]{2,1,0:T(8,128)S(1)}, f32[2,72,128]{2,1,0:T(8,128)S(1)}, u32[]{:S(2)}, u32[]{:S(2)}) collective-permute-start(f32[2,72,128]{2,1,0:T(8,128)S(1)} %add_add_fusion), channel_id=1, source_target_pairs={{0,1},{1,0},{2,3},{3,2},{4,5},{5,4},{6,7},{7,6},{8,9},{9,8},{10,11... | collective-permute-start | bytes 221192 | tf_op jit(solution)/shard_map/ppermute | solution.py:346
  84.1 5.9 %collective-permute-start.9 = (f32[2,72,128]{2,1,0:T(8,128)S(1)}, f32[2,72,128]{2,1,0:T(8,128)S(1)}, u32[]{:S(2)}, u32[]{:S(2)}) collective-permute-start(f32[2,72,128]{2,1,0:T(8,128)S(1)} %add.59), channel_id=1, source_target_pairs={{0,2},{1,3},{2,0},{3,1},{4,6},{5,7},{6,4},{7,5},{8,10},{9,11},{10,... | collective-permute-start | bytes 221192 | tf_op jit(solution)/shard_map/ppermute | solution.py:346
  90.1 10.6 %collective-permute-start.10 = (f32[2,72,128]{2,1,0:T(8,128)S(1)}, f32[2,72,128]{2,1,0:T(8,128)S(1)}, u32[]{:S(2)}, u32[]{:S(2)}) collective-permute-start(f32[2,72,128]{2,1,0:T(8,128)S(1)} %add.60), channel_id=1, source_target_pairs={{0,4},{1,5},{2,6},{3,7},{4,0},{5,1},{6,2},{7,3},{8,12},{9,13},{10,... | collective-permute-start | bytes 221192 | tf_op jit(solution)/shard_map/ppermute | solution.py:346

commit v2 on v1

v2 whole, which is shorter than its diff:
```python
import math

import jax
import jax.numpy as jnp
from jax import lax
from jax.experimental import pallas as pl
from jax.experimental.pallas import tpu as pltpu
from jax.sharding import PartitionSpec as P

CORRECTION_GAIN = 0.1
LOSS_GAIN = 8.0
SPEED_X = 0.2
DIFFUSE_X = 0.25
SPEED_Y = 0.15
SPEED_Z = 0.1
KEEP = 1.0 - SPEED_X - 2.0 * DIFFUSE_X - SPEED_Y - SPEED_Z

F32 = jnp.float32
BF16 = jnp.bfloat16

STEPS = 8
C = 8
H = 64
FEATS = 64
LANES = 128
NX = 64
NY = 8
NZ = 128
ROW = NX * NY
TILES = ROW // LANES
SLABS = 16
OWN = NZ // SLABS
WIN = 40
OWN_AT = 16
TWIN = 24
CHUNK = WIN + TWIN
SLAB_CELLS = 32
PAIRS = WIN // 2
SEEN = 9
MIDDLE = 13
STENCIL = (0.5, 4.5, 2.5, 1.5, 0.0, 1.0, 0.0)
VMEM_LIMIT = 56 * 1024 * 1024


def prepare_kernel(slots, fields, targets, out):
    field = fields[slots[0]].T
    target = targets[slots[1]].T
    field = jnp.concatenate([field[NZ - OWN_AT :], field, field[: WIN - OWN_AT]], axis=0)
    target = jnp.concatenate([target[NZ - OWN :], target, target[: TWIN - OWN]], axis=0)
    for slab in range(SLABS):
        begin = slab * OWN
        both = jnp.concatenate(
            [field[begin : begin + WIN], target[begin : begin + TWIN]], axis=0
        )
        out[slab] = both.astype(BF16)


def roll_lanes(tile, shift):
    return pltpu.roll(tile, shift % LANES, 1)


def split(row):
    return [row[:, LANES * t : LANES * (t + 1)] for t in range(TILES)]


def join(tiles):
    return jnp.concatenate(tiles, axis=1)


class Shifts:
    def __init__(self):
        lane = lax.broadcasted_iota(jnp.int32, (2 * C, LANES), 1)
        self.first_x = lane < NY
        self.last_x = lane >= LANES - NY
        self.first_y = lane % NY == 0
        self.last_y = lane % NY == NY - 1

    def x_from_below(self, row):
        rolled = [roll_lanes(t, NY) for t in split(row)]
        return join(
            [jnp.where(self.first_x, rolled[t - 1], rolled[t]) for t in range(TILES)]
        )

    def x_from_above(self, row):
        rolled = [roll_lanes(t, -NY) for t in split(row)]
        return join(
            [
                jnp.where(self.last_x, rolled[(t + 1) % TILES], rolled[t])
                for t in range(TILES)
            ]
        )

    def y_from_below(self, row):
        return join(
            [
                jnp.where(self.first_y, roll_lanes(t, 1 - NY), roll_lanes(t, 1))
                for t in split(row)
            ]
        )

    def y_from_above(self, row):
        return join(
            [
                jnp.where(self.last_y, roll_lanes(t, NY - 1), roll_lanes(t, -1))
                for t in split(row)
            ]
        )


def one_hot(shape, hit):
    rows = lax.broadcasted_iota(jnp.int32, shape, 0)
    columns = lax.broadcasted_iota(jnp.int32, shape, 1)
    return jnp.where(hit(rows, columns), 1.0, 0.0).astype(BF16)


def stencil(shape, block, other):
    rows = lax.broadcasted_iota(jnp.int32, shape, 0)
    columns = lax.broadcasted_iota(jnp.int32, shape, 1)
    which = (rows, columns)[block] // (2 * C)
    same = rows % (2 * C) == columns % (2 * C)
    value = jnp.zeros(shape, F32)
    for index, gain in enumerate(STENCIL):
        value = jnp.where(same & (which == index), gain, value)
    return value.astype(BF16)


def weave_kernel(weights, first, second, second_back, first_back):
    spread = [
        one_hot(
            (FEATS, 2 * FEATS),
            lambda r, c, s=s: c == r // C * (2 * C) + s * C + r % C,
        )
        for s in range(2)
    ]
    eye = one_hot((2 * H, 2 * H), lambda r, c: r == c)
    onto = stencil((2 * C, 2 * FEATS), 1, 0)
    back = stencil((7 * 2 * C, 2 * C), 0, 1)
    for step in range(STEPS):
        w_in = weights[step, :H, :].astype(BF16)
        rows = [jnp.dot(w_in, spread[s], preferred_element_type=F32) for s in range(2)]
        wide = jnp.concatenate(rows, axis=0).astype(BF16)
        first[step] = wide
        turned = lax.dot_general(
            eye, wide, (((1,), (1,)), ((), ())), preferred_element_type=F32
        ).astype(BF16)
        first_back[step, :, pl.ds(0, 2 * H)] = turned[: 7 * 2 * C]
        first_back[step, :, pl.ds(2 * H, 2 * C)] = back
        w_out = weights[step, H : H + C, :]
        none = jnp.zeros_like(w_out)
        left = jnp.dot(
            jnp.concatenate([w_out, none], axis=0).astype(BF16),
            one_hot((H, 2 * H), lambda r, c: r == c),
            preferred_element_type=F32,
        )
        right = jnp.dot(
            jnp.concatenate([none, w_out], axis=0).astype(BF16),
            one_hot((H, 2 * H), lambda r, c: r + H == c),
            preferred_element_type=F32,
        )
        both = (left + right).astype(BF16)
        second[step, :, pl.ds(0, 2 * H)] = both
        second[step, :, pl.ds(2 * H, 2 * FEATS)] = onto
        second_back[step] = lax.dot_general(
            eye, both, (((1,), (1,)), ((), ())), preferred_element_type=F32
        ).astype(BF16)


def rollout_kernel(
    received, first, second, second_back, first_back, out,
    unpack, state, last, target, slopes, inputs, cots,
):
    shifts = Shifts()
    lane = lax.broadcasted_iota(jnp.int32, (16, LANES), 1) // SLAB_CELLS
    low_bit = lane % 2 == 0
    high_bit = lane < 2

    for quarter in range(CHUNK // 16):
        for half in range(2):
            for tile in range(TILES):
                v = [
                    received[
                        4 * tile + a,
                        pl.ds(16 * quarter, 16),
                        pl.ds(LANES * half, LANES),
                    ].astype(F32)
                    for a in range(4)
                ]
                t = [None] * 4
                for a in (0, 2):
                    t[a] = jnp.where(low_bit, v[a], roll_lanes(v[a + 1], SLAB_CELLS))
                    t[a + 1] = jnp.where(low_bit, roll_lanes(v[a], -SLAB_CELLS), v[a + 1])
                o = [None] * 4
                for b in (0, 1):
                    o[b] = jnp.where(high_bit, t[b], roll_lanes(t[b + 2], 2 * SLAB_CELLS))
                    o[b + 2] = jnp.where(
                        high_bit, roll_lanes(t[b], -2 * SLAB_CELLS), t[b + 2]
                    )
                for b in range(4):
                    unpack[tile, pl.ds((4 * half + b) * CHUNK + 16 * quarter, 16), :] = o[b]

    def plane(at):
        return join([unpack[t, pl.ds(at, C, stride=CHUNK), :] for t in range(TILES)])

    def swapped(pair):
        return jnp.concatenate([pair[C:], pair[:C]], axis=0)

    for p in range(PAIRS):
        pair = jnp.concatenate([plane(p), plane(WIN - 1 - p)], axis=0)
        state[0, p] = pair.astype(BF16)
        if p == PAIRS - 1:
            state[0, PAIRS] = swapped(pair).astype(BF16)
    state[1, 1] = state[0, 1]
    for p in range(SEEN, PAIRS):
        target[p - SEEN] = jnp.concatenate(
            [plane(WIN + p - SEEN + 1), plane(CHUNK - 2 - p + SEEN)], axis=0
        )

    def forward_step(step, begin, kept):
        now, then = step % 2, (step + 1) % 2
        pairs = {p: state[now, p] for p in range(begin - 1, PAIRS + 1)}
        columns = []
        for p in range(begin, PAIRS):
            u, before, after = pairs[p], pairs[p - 1], pairs[p + 1]
            columns.append(
                jnp.concatenate(
                    [
                        u,
                        shifts.x_from_below(u),
                        shifts.x_from_above(u),
                        shifts.y_from_below(u),
                        shifts.y_from_above(u),
                        jnp.concatenate([before[:C], after[C:]], axis=0),
                        jnp.concatenate([after[:C], before[C:]], axis=0),
                        jnp.ones((2 * C, ROW), BF16),
                    ],
                    axis=0,
                )
            )
        stacked = join(columns)
        act = jnp.tanh(jnp.dot(first[step], stacked, preferred_element_type=F32))
        both = jnp.concatenate([act.astype(BF16), stacked], axis=0)
        after = CORRECTION_GAIN * jnp.dot(second[step], both, preferred_element_type=F32)
        seen = act[:, ROW * (kept - begin) :]
        slopes[step, :, pl.ds(ROW * (kept - SEEN), ROW * (PAIRS - kept))] = (
            1.0 - seen * seen
        ).astype(BF16)
        inputs[step] = both[:, ROW * (PAIRS - OWN // 2 - begin) :]
        for p in range(begin, PAIRS):
            at = ROW * (p - begin)
            pair = after[:, at : at + ROW]
            state[then, p] = pair.astype(BF16)
            if p >= SEEN:
                last[p - SEEN] = pair
            if p == PAIRS - 1:
                state[then, PAIRS] = swapped(pair).astype(BF16)

    for step in range(STEPS):
        forward_step(step, step + 2, max(SEEN, PAIRS - OWN // 2 - step))

    loss_scale = LOSS_GAIN / math.sqrt(16 * C * NX * NY * NZ)
    for p in range(SEEN, PAIRS):
        cots[STEPS % 2, p - SEEN] = (
            (CORRECTION_GAIN * loss_scale) * (last[p - SEEN] - target[p - SEEN])
        ).astype(BF16)

    left_half = lax.broadcasted_iota(jnp.int32, (FEATS + C, LANES), 1) < H

    def gather_grads(grad):
        rows = []
        for block in range(FEATS // C):
            at = 2 * H + 2 * C * block
            rows.append(grad[at : at + C, : 2 * H] + roll_lanes(grad[at + C : at + 2 * C, : 2 * H], -H))
        hidden = grad[: 2 * H, 2 * H :].T
        rows.append(hidden[:C] + roll_lanes(hidden[C:], -H))
        return jnp.concatenate(rows, axis=0)

    def backward_step(step, begin):
        now, then = (step + 1) % 2, step % 2
        count = PAIRS - begin
        cot = join([cots[now, p - SEEN] for p in range(begin, PAIRS)])
        cot_hidden = jnp.dot(second_back[step], cot, preferred_element_type=F32)
        slope = slopes[step, :, pl.ds(ROW * (begin - SEEN), ROW * count)]
        cot_pre = cot_hidden.astype(BF16) * slope
        both = jnp.concatenate([cot_pre, cot], axis=0)
        spread = jnp.dot(first_back[step], both, preferred_element_type=F32)
        grad = lax.dot_general(
            inputs[step],
            both[:, ROW * (count - OWN // 2) :],
            (((1,), (1,)), ((), ())),
            preferred_element_type=F32,
        )

        def part(block, p):
            at = ROW * (p - begin)
            return spread[2 * C * block : 2 * C * (block + 1), at : at + ROW]

        for p in range(begin, PAIRS):
            total = part(0, p)
            for block, shift in (
                (1, shifts.x_from_above),
                (2, shifts.x_from_below),
                (3, shifts.y_from_above),
                (4, shifts.y_from_below),
            ):
                total = total + shift(part(block, p).astype(BF16)).astype(F32)
            low, high = total[:C], total[C:]
            if p > begin:
                low = low + part(6, p - 1)[:C]
                high = high + part(5, p - 1)[C:]
            if p < PAIRS - 1:
                low = low + part(5, p + 1)[:C]
                high = high + part(6, p + 1)[C:]
            else:
                low = low + part(5, p)[C:]
                high = high + part(6, p)[:C]
            total = jnp.concatenate([low, high], axis=0)
            cots[then, p - SEEN] = (CORRECTION_GAIN * total).astype(BF16)

        summed = gather_grads(grad)
        if step % 2 == 1:
            out[step // 2] = roll_lanes(summed, H)
        else:
            out[step // 2] = jnp.where(left_half, summed, out[step // 2])

    for step in reversed(range(STEPS)):
        backward_step(step, PAIRS - OWN // 2 - step)


def vmem():
    return pl.BlockSpec(memory_space=pltpu.VMEM)


def prepare(slots, fields, targets):
    return pl.pallas_call(
        prepare_kernel,
        out_shape=jax.ShapeDtypeStruct((SLABS, CHUNK, C * SLAB_CELLS), BF16),
        in_specs=[pl.BlockSpec(memory_space=pltpu.SMEM), vmem(), vmem()],
        out_specs=vmem(),
        compiler_params=pltpu.CompilerParams(vmem_limit_bytes=VMEM_LIMIT),
        name="prepare",
    )(slots, fields, targets)


def weave(weights):
    return pl.pallas_call(
        weave_kernel,
        out_shape=(
            jax.ShapeDtypeStruct((STEPS, 2 * H, 2 * FEATS), BF16),
            jax.ShapeDtypeStruct((STEPS, 2 * C, 2 * H + 2 * FEATS), BF16),
            jax.ShapeDtypeStruct((STEPS, 2 * H, 2 * C), BF16),
            jax.ShapeDtypeStruct((STEPS, 7 * 2 * C, 2 * H + 2 * C), BF16),
        ),
        in_specs=[vmem()],
        out_specs=(vmem(),) * 4,
        compiler_params=pltpu.CompilerParams(vmem_limit_bytes=VMEM_LIMIT),
        name="weave",
    )(weights)


def rollout(received, woven):
    own = OWN // 2 * ROW
    seen = PAIRS - SEEN
    return pl.pallas_call(
        rollout_kernel,
        out_shape=jax.ShapeDtypeStruct((STEPS // 2, FEATS + C, LANES), F32),
        in_specs=[vmem()] * 5,
        out_specs=vmem(),
        scratch_shapes=[
            pltpu.VMEM((TILES, C * CHUNK, LANES), F32),
            pltpu.VMEM((2, PAIRS + 1, 2 * C, ROW), BF16),
            pltpu.VMEM((seen, 2 * C, ROW), F32),
            pltpu.VMEM((seen, 2 * C, ROW), F32),
            pltpu.VMEM((STEPS, 2 * H, seen * ROW), BF16),
            pltpu.VMEM((STEPS, 2 * H + 2 * FEATS, own), BF16),
            pltpu.VMEM((2, seen, 2 * C, ROW), BF16),
        ],
        compiler_params=pltpu.CompilerParams(vmem_limit_bytes=VMEM_LIMIT),
        name="rollout",
    )(received, *woven)


def swap(block, axis, distance):
    devices = lax.axis_size(axis)
    return lax.ppermute(block, axis, [(i, i ^ distance) for i in range(devices)])


def exchange_sum(block, axis, distances):
    arrived = [swap(block, axis, d) for d in distances]
    for other in arrived:
        block = block + other
    return block


def all_weights(weight_in, bias_in, weight_out, section):
    depth = weight_in.shape[0]
    packed = jnp.concatenate(
        [jnp.pad(weight_in, ((0, 0), (0, 0), (0, FEATS - 7 * C))), weight_out], axis=1
    ).astype(BF16)
    other = swap(packed, "section", 1)
    mine, other = packed.astype(F32), other.astype(F32)
    first = section == 0
    whole = jnp.concatenate(
        [jnp.where(first, mine, other), jnp.where(first, other, mine)], axis=0
    )
    high = lax.reduce_precision(bias_in, 8, 7)
    middle = lax.reduce_precision(bias_in - high, 8, 7)
    low = bias_in - high - middle
    columns = jnp.stack([high, middle, low], axis=2)
    columns = jnp.pad(columns, ((0, 0), (0, C), (7 * C, FEATS - 7 * C - 3)))
    return jnp.pad(whole + columns, ((0, 0), (0, C), (0, 0)))


def body(fields, targets, weight_in, bias_in, weight_out, batch_order):
    section = lax.axis_index("section")
    members = fields.shape[0]
    depth = weight_in.shape[0]
    slots = jnp.stack([section, batch_order[section]]).astype(jnp.int32)
    flat = (members, C * SLAB_CELLS, NZ)
    windows = prepare(slots, fields.reshape(flat), targets.reshape(flat))
    weights = all_weights(weight_in, bias_in, weight_out, section)
    received = lax.all_to_all(windows, "gx", 0, 0, tiled=True)
    grads = rollout(received, weave(weights))
    pairs = depth // 2
    mine = lax.dynamic_slice_in_dim(grads, section * pairs, pairs, 0)
    yours = lax.dynamic_slice_in_dim(grads, (1 - section) * pairs, pairs, 0)
    total = mine + swap(yours, "section", 1)
    total = exchange_sum(total, "gx", (1, 2, 3))
    total = exchange_sum(total, "gx", (4, 8, 12))
    for distance in (1, 2, 4):
        total = exchange_sum(total, "dp", (distance,))
    total = total.reshape(pairs, FEATS + C, 2, H).transpose(0, 2, 1, 3)
    total = total.reshape(depth, FEATS + C, H)
    grad_in = total[:, : 7 * C].transpose(0, 2, 1)
    return (grad_in, total[:, 7 * C], total[:, FEATS:])


def solution(mesh):
    return jax.shard_map(
        body,
        mesh=mesh,
        in_specs=(
            P("dp", None, "gx", None, None),
            P("dp", None, "gx", None, None),
            P("section", None, None),
            P(),
            P("section", None, None),
            P(),
        ),
        out_specs=(P("section", None, None), P("section", None), P("section", None, None)),
        check_vma=False,
    )
```

time: 103 us -> 82.9 us (0.80)
  Pallas kernels: 40 us -> 23.2 us
  waiting for transfers between devices: 23.1 us -> 19.8 us
    pallas_call x1, Pallas kernels: 38.1 us -> 17.9 us  [rollout(): pl.pallas_call(rollout_kernel, out_shape=jax.ShapeDtypeStruct((STEPS // 2...]
    all_to_all x1, waiting for transfers between devices: 5.92 us -> 2.61 us  [body(): received = lax.all_to_all(windows, 'gx', 0, 0, tiled=True)]
    pallas_call x0 -> x1, Pallas kernels: none -> 3.3 us  [weave(): pl.pallas_call(weave_kernel, out_shape=(jax.ShapeDtypeStruct((STEPS, 2 *...]
    unnamed x13 -> x12, local copies, waits for them, and re-layouts: 3.37 us -> 2.63 us
  transfers between devices with their start and end apart: 12 -> 12, of which waited for: 11 -> 11; matrix products, arithmetic and copies ran while one was open for 1% -> 1% of each run, Pallas kernels for 0% -> 4%
where the time goes in v2:
time: 82.9 us; the launch traced here: 82.5 us
  starting transfers between devices  30.1 us (36%)
  Pallas kernels  23.2 us (28%)
  waiting for transfers between devices  19.8 us (24%)
  local copies, waits for them, and re-layouts  7.1 us (9%)
  other arithmetic  1.54 us (2%)
    ppermute x11, starting transfers between devices, swap(): lax.ppermute(block, axis, [(i, i ^ distance) for i in range(devices)])  22.6 us
    pallas_call x1, Pallas kernels, rollout(): pl.pallas_call(rollout_kernel, out_shape=jax.ShapeDtypeStruct((STEPS // 2...  17.9 us
    ppermute x11, waiting for transfers between devices, swap(): lax.ppermute(block, axis, [(i, i ^ distance) for i in range(devices)])  17.2 us
    all_to_all x1, starting transfers between devices, body(): received = lax.all_to_all(windows, 'gx', 0, 0, tiled=True)  7.52 us
    pallas_call x1, Pallas kernels, weave(): pl.pallas_call(weave_kernel, out_shape=(jax.ShapeDtypeStruct((STEPS, 2 *...  3.3 us
    unnamed x12, local copies, waits for them, and re-layouts  2.63 us
    all_to_all x1, waiting for transfers between devices, body(): received = lax.all_to_all(windows, 'gx', 0, 0, tiled=True)  2.61 us
    pallas_call x1, Pallas kernels, prepare(): pl.pallas_call(prepare_kernel, out_shape=jax.ShapeDtypeStruct((SLABS, CHU...  1.95 us
  transfers between devices with their start and end apart: 12, of which 11 were waited for; matrix products, arithmetic and copies ran while one was open for 1% of the time, Pallas kernels for 4%

profile of v2, /device:TPU:8, one launch (start us, length us, event | category | flops | bytes accessed | tf_op | source)
XLA Modules:
  0.0 82.5 jit_solution(13097211617500185675)
XLA Ops:
  0.6 0.0 copy-start.5
  0.6 0.6 copy-done.5
  1.3 0.6 dynamic_slice.9
  1.9 1.2 %pad_add_fusion.slots = s32[2]{0:T(128)} fusion(s32[1]{0:T(128)} %dynamic_slice.9, s32[1]{0:T(128)} %bitcast), kind=kLoop, calls=%fused_computation.17 | loop fusion | flops 2 | bytes 16 | tf_op jit(solution)/shard_map/stack | solution.py:417
  3.1 2.0 %prepare.1 = bf16[16,64,256]{2,1,0:T(8,128)(2,1)} custom-call(s32[2]{0:T(128)} %pad_add_fusion.slots, f32[2,256,128]{2,1,0:T(8,128)} %bitcast.16, f32[2,256,128]{2,1,0:T(8,128)} %bitcast.17), custom_call_target="tpu_custom_call" | custom-call | tf_op jit(solution)/shard_map/prepare/pallas_call | solution.py:334
  5.1 0.0 copy-start.2
  5.1 7.5 %all-to-all-start = ((bf16[16,64,256]{2,1,0:T(8,128)(2,1)}), bf16[16,64,256]{2,1,0:T(8,128)(2,1)S(1)}, u32[]{:S(2)}, u32[]{:S(2)}) async-start(bf16[16,64,256]{2,1,0:T(8,128)(2,1)} %prepare.1), calls=%async_computation | async-start | bytes 1048576 | tf_op jit(solution)/shard_map/all_to_all | solution.py:421
  12.6 0.0 copy-done.2
  12.6 0.0 copy-start.3
  12.6 0.1 copy.24
  12.7 0.6 copy-done.3
  13.3 0.0 copy-start.4
  13.4 0.1 collective-permute-start
  13.5 0.6 copy-done.4
  14.0 0.1 copy.25
  14.2 0.5 collective-permute-done
  14.7 0.1 maximum_add_fusion
  14.9 0.8 pad.15.weights
  15.6 3.3 %weave.1 = (bf16[8,128,128]{2,1,0:T(8,128)(2,1)}, bf16[8,16,256]{2,1,0:T(8,128)(2,1)}, bf16[8,128,16]{2,1,0:T(8,128)(2,1)}, bf16[8,112,144]{2,1,0:T(8,128)(2,1)}) custom-call(f32[8,80,64]{2,1,0:T(8,128)} %pad.15.weights), custom_call_target="tpu_custom_call" | custom-call | tf_op jit(solution)/shard_map/weave/pallas_call | solution.py:345
  18.9 2.6 %all-to-all-done.received = bf16[16,64,256]{2,1,0:T(8,128)(2,1)S(1)} async-done(((bf16[16,64,256]{2,1,0:T(8,128)(2,1)}), bf16[16,64,256]{2,1,0:T(8,128)(2,1)S(1)}, u32[]{:S(2)}, u32[]{:S(2)}) %all-to-all-start) | async-done | bytes 524320 | tf_op jit(solution)/shard_map/all_to_all | solution.py:421
  21.5 0.0 copy-start
  21.5 0.8 copy-done
  22.4 17.9 %rollout.1 = f32[4,72,128]{2,1,0:T(8,128)} custom-call(bf16[16,64,256]{2,1,0:T(8,128)(2,1)} %copy-done, bf16[8,128,128]{2,1,0:T(8,128)(2,1)} %get-tuple-element.7.first, bf16[8,16,256]{2,1,0:T(8,128)(2,1)} %get-tuple-element.8.second, bf16[8,128,16]{2,1,0:T(8,128)(2,1)} %get-tuple-element.9.second_back, bf16[8,112,144]{2,1,0:T(8,128)(2,1)} %get-tuple-element.10.first_back), custom_call_target="tpu_custom_call" | custom-call | tf_op jit(solution)/shard_map/rollout/pallas_call | solution.py:363
  40.3 0.0 copy-start.1
  40.3 1.0 %constant_dynamic-slice_fusion = f32[2,72,128]{2,1,0:T(8,128)S(1)} fusion(f32[4,72,128]{2,1,0:T(8,128)} %rollout.1, s32[]{:T(128)S(6)} %select_n.26), kind=kLoop, calls=%fused_computation.18 | loop fusion | bytes 147460 | tf_op jit(solution)/shard_map/dynamic_slice | solution.py:425
  41.2 0.0 collective-permute-start.1
  41.2 1.3 %collective-permute-done.1 = f32[2,72,128]{2,1,0:T(8,128)S(1)} collective-permute-done((f32[2,72,128]{2,1,0:T(8,128)S(1)}, f32[2,72,128]{2,1,0:T(8,128)S(1)}, u32[]{:S(2)}, u32[]{:S(2)}) %collective-permute-start.1) | collective-permute-done | bytes 73760 | tf_op jit(solution)/shard_map/ppermute | solution.py:384
  42.5 0.0 copy-done.1
  42.5 1.8 %collective-permute-start.4 = (f32[2,72,128]{2,1,0:T(8,128)S(1)}, f32[2,72,128]{2,1,0:T(8,128)S(1)}, u32[]{:S(2)}, u32[]{:S(2)}) collective-permute-start(f32[2,72,128]{2,1,0:T(8,128)S(1)} %dynamic-slice_add_fusion), channel_id=1, source_target_pairs={{0,24},{8,16},{16,8},{24,0},{32,56},{40,48},{48,40},{56,32},{64,88... | collective-permute-start | bytes 221192 | tf_op jit(solution)/shard_map/ppermute | solution.py:384
  44.3 1.1 %collective-permute-start.3 = (f32[2,72,128]{2,1,0:T(8,128)S(1)}, f32[2,72,128]{2,1,0:T(8,128)S(1)}, u32[]{:S(2)}, u32[]{:S(2)}) collective-permute-start(f32[2,72,128]{2,1,0:T(8,128)S(1)} %dynamic-slice_add_fusion), channel_id=1, source_target_pairs={{0,16},{8,24},{16,0},{24,8},{32,48},{40,56},{48,32},{56,40},{64,80... | collective-permute-start | bytes 221192 | tf_op jit(solution)/shard_map/ppermute | solution.py:384
  45.4 1.3 %collective-permute-start.2 = (f32[2,72,128]{2,1,0:T(8,128)S(1)}, f32[2,72,128]{2,1,0:T(8,128)S(1)}, u32[]{:S(2)}, u32[]{:S(2)}) collective-permute-start(f32[2,72,128]{2,1,0:T(8,128)S(1)} %dynamic-slice_add_fusion), channel_id=1, source_target_pairs={{0,8},{8,0},{16,24},{24,16},{32,40},{40,32},{48,56},{56,48},{64,72... | collective-permute-start | bytes 221192 | tf_op jit(solution)/shard_map/ppermute | solution.py:384
  46.7 1.5 %collective-permute-done.4 = f32[2,72,128]{2,1,0:T(8,128)S(1)} collective-permute-done((f32[2,72,128]{2,1,0:T(8,128)S(1)}, f32[2,72,128]{2,1,0:T(8,128)S(1)}, u32[]{:S(2)}, u32[]{:S(2)}) %collective-permute-start.4) | collective-permute-done | bytes 73760 | tf_op jit(solution)/shard_map/ppermute | solution.py:384
  48.2 2.5 %collective-permute-done.3 = f32[2,72,128]{2,1,0:T(8,128)S(1)} collective-permute-done((f32[2,72,128]{2,1,0:T(8,128)S(1)}, f32[2,72,128]{2,1,0:T(8,128)S(1)}, u32[]{:S(2)}, u32[]{:S(2)}) %collective-permute-start.3) | collective-permute-done | bytes 73760 | tf_op jit(solution)/shard_map/ppermute | solution.py:384
  50.7 0.0 collective-permute-done.2
  50.7 1.2 %collective-permute-start.7 = (f32[2,72,128]{2,1,0:T(8,128)S(1)}, f32[2,72,128]{2,1,0:T(8,128)S(1)}, u32[]{:S(2)}, u32[]{:S(2)}) collective-permute-start(f32[2,72,128]{2,1,0:T(8,128)S(1)} %add_add_fusion.1), channel_id=1, source_target_pairs={{0,96},{8,104},{16,112},{24,120},{32,64},{40,72},{48,80},{56,88},{... | collective-permute-start | bytes 221192 | tf_op jit(solution)/shard_map/ppermute | solution.py:384
  51.9 3.3 %collective-permute-start.6 = (f32[2,72,128]{2,1,0:T(8,128)S(1)}, f32[2,72,128]{2,1,0:T(8,128)S(1)}, u32[]{:S(2)}, u32[]{:S(2)}) collective-permute-start(f32[2,72,128]{2,1,0:T(8,128)S(1)} %add_add_fusion.1), channel_id=1, source_target_pairs={{0,64},{8,72},{16,80},{24,88},{32,96},{40,104},{48,112},{56,120},{... | collective-permute-start | bytes 221192 | tf_op jit(solution)/shard_map/ppermute | solution.py:384
  55.1 0.0 collective-permute-start.5
  55.1 0.8 collective-permute-done.7
  55.9 1.8 %collective-permute-done.6 = f32[2,72,128]{2,1,0:T(8,128)S(1)} collective-permute-done((f32[2,72,128]{2,1,0:T(8,128)S(1)}, f32[2,72,128]{2,1,0:T(8,128)S(1)}, u32[]{:S(2)}, u32[]{:S(2)}) %collective-permute-start.6) | collective-permute-done | bytes 73760 | tf_op jit(solution)/shard_map/ppermute | solution.py:384
  57.7 1.8 %collective-permute-done.5 = f32[2,72,128]{2,1,0:T(8,128)S(1)} collective-permute-done((f32[2,72,128]{2,1,0:T(8,128)S(1)}, f32[2,72,128]{2,1,0:T(8,128)S(1)}, u32[]{:S(2)}, u32[]{:S(2)}) %collective-permute-start.5) | collective-permute-done | bytes 73760 | tf_op jit(solution)/shard_map/ppermute | solution.py:384
  59.5 2.0 %collective-permute-start.8 = (f32[2,72,128]{2,1,0:T(8,128)S(1)}, f32[2,72,128]{2,1,0:T(8,128)S(1)}, u32[]{:S(2)}, u32[]{:S(2)}) collective-permute-start(f32[2,72,128]{2,1,0:T(8,128)S(1)} %add_add_fusion), channel_id=1, source_target_pairs={{0,1},{1,0},{2,3},{3,2},{4,5},{5,4},{6,7},{7,6},{8,9},{9,8},{10,11... | collective-permute-start | bytes 221192 | tf_op jit(solution)/shard_map/ppermute | solution.py:384
  61.5 2.4 %collective-permute-done.8 = f32[2,72,128]{2,1,0:T(8,128)S(1)} collective-permute-done((f32[2,72,128]{2,1,0:T(8,128)S(1)}, f32[2,72,128]{2,1,0:T(8,128)S(1)}, u32[]{:S(2)}, u32[]{:S(2)}) %collective-permute-start.8) | collective-permute-done | bytes 73760 | tf_op jit(solution)/shard_map/ppermute | solution.py:384
  64.0 3.5 %collective-permute-start.9 = (f32[2,72,128]{2,1,0:T(8,128)S(1)}, f32[2,72,128]{2,1,0:T(8,128)S(1)}, u32[]{:S(2)}, u32[]{:S(2)}) collective-permute-start(f32[2,72,128]{2,1,0:T(8,128)S(1)} %add.59), channel_id=1, source_target_pairs={{0,2},{1,3},{2,0},{3,1},{4,6},{5,7},{6,4},{7,5},{8,10},{9,11},{10,... | collective-permute-start | bytes 221192 | tf_op jit(solution)/shard_map/ppermute | solution.py:384
  67.5 2.3 %collective-permute-done.9 = f32[2,72,128]{2,1,0:T(8,128)S(1)} collective-permute-done((f32[2,72,128]{2,1,0:T(8,128)S(1)}, f32[2,72,128]{2,1,0:T(8,128)S(1)}, u32[]{:S(2)}, u32[]{:S(2)}) %collective-permute-start.9) | collective-permute-done | bytes 73760 | tf_op jit(solution)/shard_map/ppermute | solution.py:384
  69.9 8.3 %collective-permute-start.10 = (f32[2,72,128]{2,1,0:T(8,128)S(1)}, f32[2,72,128]{2,1,0:T(8,128)S(1)}, u32[]{:S(2)}, u32[]{:S(2)}) collective-permute-start(f32[2,72,128]{2,1,0:T(8,128)S(1)} %add.60), channel_id=1, source_target_pairs={{0,4},{1,5},{2,6},{3,7},{4,0},{5,1},{6,2},{7,3},{8,12},{9,13},{10,... | collective-permute-start | bytes 221192 | tf_op jit(solution)/shard_map/ppermute | solution.py:384
  78.2 2.3 %collective-permute-done.10 = f32[2,72,128]{2,1,0:T(8,128)S(1)} collective-permute-done((f32[2,72,128]{2,1,0:T(8,128)S(1)}, f32[2,72,128]{2,1,0:T(8,128)S(1)}, u32[]{:S(2)}, u32[]{:S(2)}) %collective-permute-start.10) | collective-permute-done | bytes 73760 | tf_op jit(solution)/shard_map/ppermute | solution.py:384
  80.5 0.1 fusion.3
  80.6 0.7 slice_bitcast_fusion
  81.3 0.6 slice.23
  81.9 0.6 slice.24
  (13 shorter events, 0.2 us)
Async XLA Ops:
  0.6 0.7 copy-start.5
  5.1 7.5 %copy-start.2 = (f32[4,64,56]{1,2,0:T(8,128)S(1)}, f32[4,64,56]{1,2,0:T(8,128)}, u32[]{:S(2)}) copy-start(f32[4,64,56]{1,2,0:T(8,128)} %param.8) | copy-start | bytes 172036
  5.1 16.5 %all-to-all-start = ((bf16[16,64,256]{2,1,0:T(8,128)(2,1)}), bf16[16,64,256]{2,1,0:T(8,128)(2,1)S(1)}, u32[]{:S(2)}, u32[]{:S(2)}) async-start(bf16[16,64,256]{2,1,0:T(8,128)(2,1)} %prepare.1), calls=%async_computation | async-start | bytes 1048576 | tf_op jit(solution)/shard_map/all_to_all | solution.py:421
  12.6 0.7 copy-start.3
  13.3 0.7 copy-start.4
  13.4 1.4 %collective-permute-start = (bf16[4,72,64]{2,1,0:T(8,128)(2,1)S(1)}, bf16[4,72,64]{2,1,0:T(8,128)(2,1)S(1)}, u32[]{:S(2)}, u32[]{:S(2)}) collective-permute-start(bf16[4,72,64]{2,1,0:T(8,128)(2,1)S(1)} %fusion.1), channel_id=1, source_target_pairs={{0,128},{128,0},{1,129},{129,1},{2,130},{130,2},{3,131},{131,3},{4... | collective-permute-start | bytes 110600 | tf_op jit(solution)/shard_map/ppermute | solution.py:384
  21.5 0.8 copy-start
  40.3 2.2 %copy-start.1 = (f32[4,72,128]{2,1,0:T(8,128)S(1)}, f32[4,72,128]{2,1,0:T(8,128)}, u32[]{:S(2)}) copy-start(f32[4,72,128]{2,1,0:T(8,128)} %rollout.1) | copy-start | bytes 442372
  41.2 1.3 %collective-permute-start.1 = (f32[2,72,128]{2,1,0:T(8,128)S(1)}, f32[2,72,128]{2,1,0:T(8,128)S(1)}, u32[]{:S(2)}, u32[]{:S(2)}) collective-permute-start(f32[2,72,128]{2,1,0:T(8,128)S(1)} %constant_dynamic-slice_fusion), channel_id=1, source_target_pairs={{0,128},{128,0},{1,129},{129,1},{2,130},{130,2},{3,131},{131,3},{4... | collective-permute-start | bytes 221192 | tf_op jit(solution)/shard_map/ppermute | solution.py:384
  42.5 5.7 %collective-permute-start.4 = (f32[2,72,128]{2,1,0:T(8,128)S(1)}, f32[2,72,128]{2,1,0:T(8,128)S(1)}, u32[]{:S(2)}, u32[]{:S(2)}) collective-permute-start(f32[2,72,128]{2,1,0:T(8,128)S(1)} %dynamic-slice_add_fusion), channel_id=1, source_target_pairs={{0,24},{8,16},{16,8},{24,0},{32,56},{40,48},{48,40},{56,32},{64,88... | collective-permute-start | bytes 221192 | tf_op jit(solution)/shard_map/ppermute | solution.py:384
  44.3 6.3 %collective-permute-start.3 = (f32[2,72,128]{2,1,0:T(8,128)S(1)}, f32[2,72,128]{2,1,0:T(8,128)S(1)}, u32[]{:S(2)}, u32[]{:S(2)}) collective-permute-start(f32[2,72,128]{2,1,0:T(8,128)S(1)} %dynamic-slice_add_fusion), channel_id=1, source_target_pairs={{0,16},{8,24},{16,0},{24,8},{32,48},{40,56},{48,32},{56,40},{64,80... | collective-permute-start | bytes 221192 | tf_op jit(solution)/shard_map/ppermute | solution.py:384
  45.4 5.3 %collective-permute-start.2 = (f32[2,72,128]{2,1,0:T(8,128)S(1)}, f32[2,72,128]{2,1,0:T(8,128)S(1)}, u32[]{:S(2)}, u32[]{:S(2)}) collective-permute-start(f32[2,72,128]{2,1,0:T(8,128)S(1)} %dynamic-slice_add_fusion), channel_id=1, source_target_pairs={{0,8},{8,0},{16,24},{24,16},{32,40},{40,32},{48,56},{56,48},{64,72... | collective-permute-start | bytes 221192 | tf_op jit(solution)/shard_map/ppermute | solution.py:384
  50.7 5.2 %collective-permute-start.7 = (f32[2,72,128]{2,1,0:T(8,128)S(1)}, f32[2,72,128]{2,1,0:T(8,128)S(1)}, u32[]{:S(2)}, u32[]{:S(2)}) collective-permute-start(f32[2,72,128]{2,1,0:T(8,128)S(1)} %add_add_fusion.1), channel_id=1, source_target_pairs={{0,96},{8,104},{16,112},{24,120},{32,64},{40,72},{48,80},{56,88},{... | collective-permute-start | bytes 221192 | tf_op jit(solution)/shard_map/ppermute | solution.py:384
  51.9 5.9 %collective-permute-start.6 = (f32[2,72,128]{2,1,0:T(8,128)S(1)}, f32[2,72,128]{2,1,0:T(8,128)S(1)}, u32[]{:S(2)}, u32[]{:S(2)}) collective-permute-start(f32[2,72,128]{2,1,0:T(8,128)S(1)} %add_add_fusion.1), channel_id=1, source_target_pairs={{0,64},{8,72},{16,80},{24,88},{32,96},{40,104},{48,112},{56,120},{... | collective-permute-start | bytes 221192 | tf_op jit(solution)/shard_map/ppermute | solution.py:384
  55.1 4.4 %collective-permute-start.5 = (f32[2,72,128]{2,1,0:T(8,128)S(1)}, f32[2,72,128]{2,1,0:T(8,128)S(1)}, u32[]{:S(2)}, u32[]{:S(2)}) collective-permute-start(f32[2,72,128]{2,1,0:T(8,128)S(1)} %add_add_fusion.1), channel_id=1, source_target_pairs={{0,32},{8,40},{16,48},{24,56},{32,0},{40,8},{48,16},{56,24},{64,96... | collective-permute-start | bytes 221192 | tf_op jit(solution)/shard_map/ppermute | solution.py:384
  59.5 4.4 %collective-permute-start.8 = (f32[2,72,128]{2,1,0:T(8,128)S(1)}, f32[2,72,128]{2,1,0:T(8,128)S(1)}, u32[]{:S(2)}, u32[]{:S(2)}) collective-permute-start(f32[2,72,128]{2,1,0:T(8,128)S(1)} %add_add_fusion), channel_id=1, source_target_pairs={{0,1},{1,0},{2,3},{3,2},{4,5},{5,4},{6,7},{7,6},{8,9},{9,8},{10,11... | collective-permute-start | bytes 221192 | tf_op jit(solution)/shard_map/ppermute | solution.py:384
  64.0 5.9 %collective-permute-start.9 = (f32[2,72,128]{2,1,0:T(8,128)S(1)}, f32[2,72,128]{2,1,0:T(8,128)S(1)}, u32[]{:S(2)}, u32[]{:S(2)}) collective-permute-start(f32[2,72,128]{2,1,0:T(8,128)S(1)} %add.59), channel_id=1, source_target_pairs={{0,2},{1,3},{2,0},{3,1},{4,6},{5,7},{6,4},{7,5},{8,10},{9,11},{10,... | collective-permute-start | bytes 221192 | tf_op jit(solution)/shard_map/ppermute | solution.py:384
  69.9 10.7 %collective-permute-start.10 = (f32[2,72,128]{2,1,0:T(8,128)S(1)}, f32[2,72,128]{2,1,0:T(8,128)S(1)}, u32[]{:S(2)}, u32[]{:S(2)}) collective-permute-start(f32[2,72,128]{2,1,0:T(8,128)S(1)} %add.60), channel_id=1, source_target_pairs={{0,4},{1,5},{2,6},{3,7},{4,0},{5,1},{6,2},{7,3},{8,12},{9,13},{10,... | collective-permute-start | bytes 221192 | tf_op jit(solution)/shard_map/ppermute | solution.py:384

commit v3 on v2

--- a/solution.py
+++ b/solution.py
@@ -42,9 +42,10 @@
 VMEM_LIMIT = 56 * 1024 * 1024
 
 
-def prepare_kernel(slots, fields, targets, out):
-    field = fields[slots[0]].T
-    target = targets[slots[1]].T
+def prepare_kernel(order, fields, targets, out):
+    member = lax.axis_index("section")
+    field = fields[member].T
+    target = targets[order[member]].T
     field = jnp.concatenate([field[NZ - OWN_AT :], field, field[: WIN - OWN_AT]], axis=0)
     target = jnp.concatenate([target[NZ - OWN :], target, target[: TWIN - OWN]], axis=0)
     for slab in range(SLABS):
@@ -139,7 +140,8 @@
         w_in = weights[step, :H, :].astype(BF16)
         rows = [jnp.dot(w_in, spread[s], preferred_element_type=F32) for s in range(2)]
         wide = jnp.concatenate(rows, axis=0).astype(BF16)
-        first[step] = wide
+        first[step, pl.ds(0, 2 * H), :] = wide
+        first[step, pl.ds(2 * H, 2 * C), :] = onto
         turned = lax.dot_general(
             eye, wide, (((1,), (1,)), ((), ())), preferred_element_type=F32
         ).astype(BF16)
@@ -158,17 +160,17 @@
             preferred_element_type=F32,
         )
         both = (left + right).astype(BF16)
-        second[step, :, pl.ds(0, 2 * H)] = both
-        second[step, :, pl.ds(2 * H, 2 * FEATS)] = onto
+        second[step] = both
         second_back[step] = lax.dot_general(
             eye, both, (((1,), (1,)), ((), ())), preferred_element_type=F32
         ).astype(BF16)
 
 
 def rollout_kernel(
-    received, first, second, second_back, first_back, out,
-    unpack, state, last, target, slopes, inputs, cots,
+    received, first, second, second_back, first_back, mine, yours,
+    unpack, state, last, target, slopes, inputs, cots, grads,
 ):
+    section = lax.axis_index("section")
     shifts = Shifts()
     lane = lax.broadcasted_iota(jnp.int32, (16, LANES), 1) // SLAB_CELLS
     low_bit = lane % 2 == 0
@@ -182,7 +184,7 @@
                         4 * tile + a,
                         pl.ds(16 * quarter, 16),
                         pl.ds(LANES * half, LANES),
-                    ].astype(F32)
+                    ]
                     for a in range(4)
                 ]
                 t = [None] * 4
@@ -196,7 +198,9 @@
                         high_bit, roll_lanes(t[b], -2 * SLAB_CELLS), t[b + 2]
                     )
                 for b in range(4):
-                    unpack[tile, pl.ds((4 * half + b) * CHUNK + 16 * quarter, 16), :] = o[b]
+                    unpack[tile, pl.ds((4 * half + b) * CHUNK + 16 * quarter, 16), :] = o[
+                        b
+                    ].astype(F32)
 
     def plane(at):
         return join([unpack[t, pl.ds(at, C, stride=CHUNK), :] for t in range(TILES)])
@@ -237,14 +241,19 @@
                 )
             )
         stacked = join(columns)
-        act = jnp.tanh(jnp.dot(first[step], stacked, preferred_element_type=F32))
-        both = jnp.concatenate([act.astype(BF16), stacked], axis=0)
-        after = CORRECTION_GAIN * jnp.dot(second[step], both, preferred_element_type=F32)
+        mapped = jnp.dot(first[step], stacked, preferred_element_type=F32)
+        act = jnp.tanh(mapped[: 2 * H])
+        hidden = act.astype(BF16)
+        after = CORRECTION_GAIN * (
+            mapped[2 * H :] + jnp.dot(second[step], hidden, preferred_element_type=F32)
+        )
         seen = act[:, ROW * (kept - begin) :]
         slopes[step, :, pl.ds(ROW * (kept - SEEN), ROW * (PAIRS - kept))] = (
             1.0 - seen * seen
         ).astype(BF16)
-        inputs[step] = both[:, ROW * (PAIRS - OWN // 2 - begin) :]
+        own = ROW * (PAIRS - OWN // 2 - begin)
+        inputs[step, pl.ds(0, 2 * H), :] = hidden[:, own:]
+        inputs[step, pl.ds(2 * H, 2 * FEATS), :] = stacked[:, own:]
         for p in range(begin, PAIRS):
             at = ROW * (p - begin)
             pair = after[:, at : at + ROW]
@@ -318,19 +327,23 @@
 
         summed = gather_grads(grad)
         if step % 2 == 1:
-            out[step // 2] = roll_lanes(summed, H)
+            grads[step // 2] = roll_lanes(summed, H)
         else:
-            out[step // 2] = jnp.where(left_half, summed, out[step // 2])
+            grads[step // 2] = jnp.where(left_half, summed, grads[step // 2])
 
     for step in reversed(range(STEPS)):
         backward_step(step, PAIRS - OWN // 2 - step)
 
+    half = STEPS // 4
+    mine[...] = grads[pl.ds(section * half, half)]
+    yours[...] = grads[pl.ds((1 - section) * half, half)]
+
 
 def vmem():
     return pl.BlockSpec(memory_space=pltpu.VMEM)
 
 
-def prepare(slots, fields, targets):
+def prepare(order, fields, targets):
     return pl.pallas_call(
         prepare_kernel,
         out_shape=jax.ShapeDtypeStruct((SLABS, CHUNK, C * SLAB_CELLS), BF16),
@@ -338,15 +351,15 @@
         out_specs=vmem(),
         compiler_params=pltpu.CompilerParams(vmem_limit_bytes=VMEM_LIMIT),
         name="prepare",
-    )(slots, fields, targets)
+    )(order, fields, targets)
 
 
 def weave(weights):
     return pl.pallas_call(
         weave_kernel,
         out_shape=(
-            jax.ShapeDtypeStruct((STEPS, 2 * H, 2 * FEATS), BF16),
-            jax.ShapeDtypeStruct((STEPS, 2 * C, 2 * H + 2 * FEATS), BF16),
+            jax.ShapeDtypeStruct((STEPS, 2 * H + 2 * C, 2 * FEATS), BF16),
+            jax.ShapeDtypeStruct((STEPS, 2 * C, 2 * H), BF16),
             jax.ShapeDtypeStruct((STEPS, 2 * H, 2 * C), BF16),
             jax.ShapeDtypeStruct((STEPS, 7 * 2 * C, 2 * H + 2 * C), BF16),
         ),
@@ -362,9 +375,9 @@
     seen = PAIRS - SEEN
     return pl.pallas_call(
         rollout_kernel,
-        out_shape=jax.ShapeDtypeStruct((STEPS // 2, FEATS + C, LANES), F32),
+        out_shape=(jax.ShapeDtypeStruct((STEPS // 4, FEATS + C, LANES), F32),) * 2,
         in_specs=[vmem()] * 5,
-        out_specs=vmem(),
+        out_specs=(vmem(),) * 2,
         scratch_shapes=[
             pltpu.VMEM((TILES, C * CHUNK, LANES), F32),
             pltpu.VMEM((2, PAIRS + 1, 2 * C, ROW), BF16),
@@ -373,22 +386,51 @@
             pltpu.VMEM((STEPS, 2 * H, seen * ROW), BF16),
             pltpu.VMEM((STEPS, 2 * H + 2 * FEATS, own), BF16),
             pltpu.VMEM((2, seen, 2 * C, ROW), BF16),
+            pltpu.VMEM((STEPS // 2, FEATS + C, LANES), F32),
         ],
         compiler_params=pltpu.CompilerParams(vmem_limit_bytes=VMEM_LIMIT),
         name="rollout",
     )(received, *woven)
 
 
+def finish_kernel(parts, grad_in, grad_bias, grad_out):
+    total = parts[0].astype(F32)
+    for i in range(1, parts.shape[0]):
+        total = total + parts[i].astype(F32)
+    rows = FEATS + C
+    for step in range(grad_in.shape[0]):
+        at = step // 2 * rows
+        side = total[at : at + rows]
+        if step % 2:
+            side = roll_lanes(side, H)
+        grad_in[step] = side[: 7 * C, :H]
+        grad_bias[pl.ds(step, 1), :] = side[7 * C : 7 * C + 1, :H]
+        grad_out[step] = side[FEATS:, :H]
+
+
+def finish(parts, depth):
+    return pl.pallas_call(
+        finish_kernel,
+        out_shape=(
+            jax.ShapeDtypeStruct((depth, 7 * C, H), F32),
+            jax.ShapeDtypeStruct((depth, H), F32),
+            jax.ShapeDtypeStruct((depth, C, H), F32),
+        ),
+        in_specs=[vmem()],
+        out_specs=(vmem(),) * 3,
+        compiler_params=pltpu.CompilerParams(vmem_limit_bytes=VMEM_LIMIT),
+        name="finish",
+    )(parts)
+
+
 def swap(block, axis, distance):
     devices = lax.axis_size(axis)
     return lax.ppermute(block, axis, [(i, i ^ distance) for i in range(devices)])
 
 
-def exchange_sum(block, axis, distances):
-    arrived = [swap(block, axis, d) for d in distances]
-    for other in arrived:
-        block = block + other
-    return block
+def everyones(block, axis):
+    same = jnp.broadcast_to(block.astype(BF16)[None], (lax.axis_size(axis),) + block.shape)
+    return lax.all_to_all(same, axis, 0, 0, tiled=True)
 
 
 def all_weights(weight_in, bias_in, weight_out, section):
@@ -414,24 +456,19 @@
     section = lax.axis_index("section")
     members = fields.shape[0]
     depth = weight_in.shape[0]
-    slots = jnp.stack([section, batch_order[section]]).astype(jnp.int32)
     flat = (members, C * SLAB_CELLS, NZ)
-    windows = prepare(slots, fields.reshape(flat), targets.reshape(flat))
+    windows = prepare(batch_order, fields.reshape(flat), targets.reshape(flat))
+    windows, weight_in, bias_in, weight_out = lax.optimization_barrier(
+        (windows, weight_in, bias_in, weight_out)
+    )
     weights = all_weights(weight_in, bias_in, weight_out, section)
     received = lax.all_to_all(windows, "gx", 0, 0, tiled=True)
-    grads = rollout(received, weave(weights))
-    pairs = depth // 2
-    mine = lax.dynamic_slice_in_dim(grads, section * pairs, pairs, 0)
-    yours = lax.dynamic_slice_in_dim(grads, (1 - section) * pairs, pairs, 0)
+    mine, yours = rollout(received, weave(weights))
     total = mine + swap(yours, "section", 1)
-    total = exchange_sum(total, "gx", (1, 2, 3))
-    total = exchange_sum(total, "gx", (4, 8, 12))
-    for distance in (1, 2, 4):
-        total = exchange_sum(total, "dp", (distance,))
-    total = total.reshape(pairs, FEATS + C, 2, H).transpose(0, 2, 1, 3)
-    total = total.reshape(depth, FEATS + C, H)
-    grad_in = total[:, : 7 * C].transpose(0, 2, 1)
-    return (grad_in, total[:, 7 * C], total[:, FEATS:])
+    total = total.reshape(-1, LANES)
+    total = jnp.sum(everyones(total, "gx").astype(F32), axis=0)
+    grad_in, grad_bias, grad_out = finish(everyones(total, "dp"), depth)
+    return (grad_in.transpose(0, 2, 1), grad_bias, grad_out)
 
 
 def solution(mesh):

time: 82.9 us -> 78.3 us (0.945)
  blocking collectives: 0 us -> 36.7 us
  starting transfers between devices: 30.1 us -> 7.62 us
  waiting for transfers between devices: 19.8 us -> 5.17 us
  local copies, waits for them, and re-layouts: 7.1 us -> 2.48 us
    all_to_all x0 -> x2, blocking collectives: none -> 36.7 us  [everyones(): return lax.all_to_all(same, axis, 0, 0, tiled=True)]
    ppermute x11 -> x2, starting transfers between devices: 22.6 us -> 0.1 us  [swap(): lax.ppermute(block, axis, [(i, i ^ distance) for i in range(devices)])]
    ppermute x11 -> x2, waiting for transfers between devices: 17.2 us -> 2 us  [swap(): lax.ppermute(block, axis, [(i, i ^ distance) for i in range(devices)])]
    dynamic_slice x2 -> x0, local copies, waits for them, and re-layouts: 1.54 us -> none  [the longest x1 0.96 us: body(): yours = lax.dynamic_slice_in_dim(grads, (1 - section) * pairs, pairs, 0)]
    unnamed x12 -> x8, local copies, waits for them, and re-layouts: 2.63 us -> 1.35 us
    slice x3 -> x0, local copies, waits for them, and re-layouts: 1.27 us -> none  [the longest x2 1.19 us: body(): return (grad_in, total[:, 7 * C], total[:, FEATS:])]
    another operation x3 -> x2, other arithmetic: 1.24 us -> 0.01 us  [the longest x1 1.23 us: body(): slots = jnp.stack([section, batch_order[section]]).astype(jnp.int32)]
    convert_element_type x0 -> x1, other arithmetic: none -> 0.9 us  [everyones(): block.astype(BF16)[None]]
  transfers between devices with their start and end apart: 12 -> 3, of which waited for: 11 -> 3; matrix products, arithmetic and copies ran while one was open for 1% -> 2% of each run, Pallas kernels for 4% -> 4%
where the time goes in v3:
time: 78.3 us; the launch traced here: 77.9 us
  blocking collectives  36.7 us (47%)
  Pallas kernels  23.9 us (31%)
  starting transfers between devices  7.62 us (10%)
  waiting for transfers between devices  5.17 us (7%)
  local copies, waits for them, and re-layouts  2.48 us (3%)
  other arithmetic  1.19 us (2%)
    all_to_all x2, blocking collectives, everyones(): return lax.all_to_all(same, axis, 0, 0, tiled=True)  36.7 us
    pallas_call x1, Pallas kernels, rollout(): pl.pallas_call(rollout_kernel, out_shape=(jax.ShapeDtypeStruct((STEPS //...  17 us
    all_to_all x1, starting transfers between devices, body(): received = lax.all_to_all(windows, 'gx', 0, 0, tiled=True)  7.52 us
    pallas_call x1, Pallas kernels, weave(): pl.pallas_call(weave_kernel, out_shape=(jax.ShapeDtypeStruct((STEPS, 2 *...  3.31 us
    all_to_all x1, waiting for transfers between devices, body(): received = lax.all_to_all(windows, 'gx', 0, 0, tiled=True)  3.17 us
    ppermute x2, waiting for transfers between devices, swap(): lax.ppermute(block, axis, [(i, i ^ distance) for i in range(devices)])  2 us
    pallas_call x1, Pallas kernels, prepare(): pl.pallas_call(prepare_kernel, out_shape=jax.ShapeDtypeStruct((SLABS, CHU...  1.95 us
    pallas_call x1, Pallas kernels, finish(): pl.pallas_call(finish_kernel, out_shape=(jax.ShapeDtypeStruct((depth, 7 *...  1.71 us
  transfers between devices with their start and end apart: 3, of which 3 were waited for; matrix products, arithmetic and copies ran while one was open for 2% of the time, Pallas kernels for 4%

profile of v3, /device:TPU:8, one launch (start us, length us, event | category | flops | bytes accessed | tf_op | source)
XLA Modules:
  0.0 77.9 jit_solution(8640695583242813031)
XLA Ops:
  0.6 1.9 %prepare.1 = bf16[16,64,256]{2,1,0:T(8,128)(2,1)} custom-call(s32[2]{0:T(128)} %order.1, f32[2,256,128]{2,1,0:T(8,128)} %bitcast.10, f32[2,256,128]{2,1,0:T(8,128)} %bitcast.11), custom_call_target="tpu_custom_call" | custom-call | tf_op jit(solution)/shard_map/prepare/pallas_call | solution.py:347
  2.6 0.0 copy-start.2
  2.6 0.0 copy-start.1
  2.6 7.5 %all-to-all-start = ((bf16[16,64,256]{2,1,0:T(8,128)(2,1)}), bf16[16,64,256]{2,1,0:T(8,128)(2,1)S(1)}, u32[]{:S(2)}, u32[]{:S(2)}) async-start(bf16[16,64,256]{2,1,0:T(8,128)(2,1)} %prepare.1), calls=%async_computation | async-start | bytes 1048576 | tf_op jit(solution)/shard_map/all_to_all | solution.py:465
  10.1 0.0 copy-done.2
  10.1 0.0 copy-done.1
  10.2 0.1 copy.26
  10.3 0.0 copy-start.3
  10.3 0.1 collective-permute-start
  10.4 0.6 copy-done.3
  11.0 0.1 copy.27
  11.1 0.5 collective-permute-done
  11.7 0.1 maximum_add_fusion
  11.8 0.8 pad.15.weights
  12.6 3.3 %weave.1 = (bf16[8,144,128]{2,1,0:T(8,128)(2,1)}, bf16[8,16,128]{2,1,0:T(8,128)(2,1)}, bf16[8,128,16]{2,1,0:T(8,128)(2,1)}, bf16[8,112,144]{2,1,0:T(8,128)(2,1)}) custom-call(f32[8,80,64]{2,1,0:T(8,128)} %pad.15.weights), custom_call_target="tpu_custom_call" | custom-call | tf_op jit(solution)/shard_map/weave/pallas_call | solution.py:358
  15.9 3.2 %all-to-all-done.received = bf16[16,64,256]{2,1,0:T(8,128)(2,1)S(1)} async-done(((bf16[16,64,256]{2,1,0:T(8,128)(2,1)}), bf16[16,64,256]{2,1,0:T(8,128)(2,1)S(1)}, u32[]{:S(2)}, u32[]{:S(2)}) %all-to-all-start) | async-done | bytes 524320 | tf_op jit(solution)/shard_map/all_to_all | solution.py:465
  19.1 0.0 copy-start
  19.1 0.8 %copy-done = bf16[16,64,256]{2,1,0:T(8,128)(2,1)} copy-done((bf16[16,64,256]{2,1,0:T(8,128)(2,1)}, bf16[16,64,256]{2,1,0:T(8,128)(2,1)S(1)}, u32[]{:S(2)}) %copy-start) | copy-done | bytes 524312
  19.9 17.0 %rollout.1 = (f32[2,72,128]{2,1,0:T(8,128)}, f32[2,72,128]{2,1,0:T(8,128)}) custom-call(bf16[16,64,256]{2,1,0:T(8,128)(2,1)} %copy-done, bf16[8,144,128]{2,1,0:T(8,128)(2,1)} %get-tuple-element.20.first, bf16[8,16,128]{2,1,0:T(8,128)(2,1)} %get-tuple-element.21.second, bf16[8,128,16]{2,1,0:T(8,128)(2,1)} %get-tuple-element.22.second_back, ...), custom_call_target="tpu_custom_call" | custom-call | tf_op jit(solution)/shard_map/rollout/pallas_call | solution.py:376
  36.8 0.0 collective-permute-start.1
  36.8 1.5 %collective-permute-done.1 = f32[2,72,128]{2,1,0:T(8,128)S(1)} collective-permute-done((f32[2,72,128]{2,1,0:T(8,128)}, f32[2,72,128]{2,1,0:T(8,128)S(1)}, u32[]{:S(2)}, u32[]{:S(2)}) %collective-permute-start.1) | collective-permute-done | bytes 73760 | tf_op jit(solution)/shard_map/ppermute | solution.py:428
  38.3 0.9 %add_convert_fusion = bf16[2,72,128]{2,1,0:T(8,128)(2,1)S(1)} fusion(f32[2,72,128]{2,1,0:T(8,128)} %get-tuple-element.24, f32[2,72,128]{2,1,0:T(8,128)S(1)} %collective-permute-done.1), kind=kLoop, calls=%fused_computation.6 | loop fusion | flops 36864 | bytes 184320 | tf_op jit(solution)/shard_map/convert_element_type | solution.py:432
  39.2 0.1 broadcast_in_dim.4
  39.3 16.7 %all_to_all.15 = bf16[16,144,128]{2,1,0:T(8,128)(2,1)S(1)} all-to-all(bf16[16,144,128]{2,1,0:T(8,128)(2,1)S(1)} %broadcast_in_dim.4), channel_id=1, replica_groups=mesh['section'=2,'gx'=16,'dp'=8] {'gx'}, dimensions={0} | all-to-all | bytes 1179648 | tf_op jit(solution)/shard_map/all_to_all | solution.py:433
  56.0 0.1 reduce_sum.12
  56.1 20.0 %all_to_all.16.parts = bf16[8,144,128]{2,1,0:T(8,128)(2,1)} all-to-all(bf16[8,144,128]{2,1,0:T(8,128)(2,1)S(1)} %broadcast_in_dim.5), channel_id=1, replica_groups=mesh['section'=2,'gx'=16,'dp'=8] {'dp'}, dimensions={0} | all-to-all | bytes 589824 | tf_op jit(solution)/shard_map/all_to_all | solution.py:433
  76.2 1.7 %finish.1 = (f32[4,56,64]{2,1,0:T(8,128)}, f32[4,64]{1,0:T(4,128)}, f32[4,8,64]{2,1,0:T(8,128)}) custom-call(bf16[8,144,128]{2,1,0:T(8,128)(2,1)} %all_to_all.16.parts), custom_call_target="tpu_custom_call" | custom-call | tf_op jit(solution)/shard_map/finish/pallas_call | solution.py:412
  (7 shorter events, 0.1 us)
Async XLA Ops:
  2.6 7.5 %copy-start.2 = (f32[4,8,64]{2,1,0:T(8,128)S(1)}, f32[4,8,64]{2,1,0:T(8,128)}, u32[]{:S(2)}) copy-start(f32[4,8,64]{2,1,0:T(8,128)} %param.10) | copy-start | bytes 24580
  2.6 7.5 %copy-start.1 = (f32[4,64,56]{1,2,0:T(8,128)S(1)}, f32[4,64,56]{1,2,0:T(8,128)}, u32[]{:S(2)}) copy-start(f32[4,64,56]{1,2,0:T(8,128)} %param.8) | copy-start | bytes 172036
  2.6 16.5 %all-to-all-start = ((bf16[16,64,256]{2,1,0:T(8,128)(2,1)}), bf16[16,64,256]{2,1,0:T(8,128)(2,1)S(1)}, u32[]{:S(2)}, u32[]{:S(2)}) async-start(bf16[16,64,256]{2,1,0:T(8,128)(2,1)} %prepare.1), calls=%async_computation | async-start | bytes 1048576 | tf_op jit(solution)/shard_map/all_to_all | solution.py:465
  10.3 0.7 copy-start.3
  10.3 1.4 %collective-permute-start = (bf16[4,72,64]{2,1,0:T(8,128)(2,1)S(1)}, bf16[4,72,64]{2,1,0:T(8,128)(2,1)S(1)}, u32[]{:S(2)}, u32[]{:S(2)}) collective-permute-start(bf16[4,72,64]{2,1,0:T(8,128)(2,1)S(1)} %fusion.1), channel_id=1, source_target_pairs={{0,128},{128,0},{1,129},{129,1},{2,130},{130,2},{3,131},{131,3},{4... | collective-permute-start | bytes 110600 | tf_op jit(solution)/shard_map/ppermute | solution.py:428
  19.1 0.8 %copy-start = (bf16[16,64,256]{2,1,0:T(8,128)(2,1)}, bf16[16,64,256]{2,1,0:T(8,128)(2,1)S(1)}, u32[]{:S(2)}) copy-start(bf16[16,64,256]{2,1,0:T(8,128)(2,1)S(1)} %all-to-all-done.received) | copy-start | bytes 1572868
  36.8 1.5 %collective-permute-start.1 = (f32[2,72,128]{2,1,0:T(8,128)}, f32[2,72,128]{2,1,0:T(8,128)S(1)}, u32[]{:S(2)}, u32[]{:S(2)}) collective-permute-start(f32[2,72,128]{2,1,0:T(8,128)} %get-tuple-element.25), channel_id=1, source_target_pairs={{0,128},{128,0},{1,129},{129,1},{2,130},{130,2},{3,131},{131,3},{4... | collective-permute-start | bytes 221192 | tf_op jit(solution)/shard_map/ppermute | solution.py:428

commit v4 on v3

--- a/solution.py
+++ b/solution.py
@@ -39,7 +39,8 @@
 SEEN = 9
 MIDDLE = 13
 STENCIL = (0.5, 4.5, 2.5, 1.5, 0.0, 1.0, 0.0)
-VMEM_LIMIT = 56 * 1024 * 1024
+MIB = 1024 * 1024
+VMEM_LIMIT = 56 * MIB
 
 
 def prepare_kernel(order, fields, targets, out):
@@ -292,12 +293,8 @@
         cot_pre = cot_hidden.astype(BF16) * slope
         both = jnp.concatenate([cot_pre, cot], axis=0)
         spread = jnp.dot(first_back[step], both, preferred_element_type=F32)
-        grad = lax.dot_general(
-            inputs[step],
-            both[:, ROW * (count - OWN // 2) :],
-            (((1,), (1,)), ((), ())),
-            preferred_element_type=F32,
-        )
+        turned = both[:, ROW * (count - OWN // 2) :].astype(F32).T.astype(BF16)
+        grad = jnp.dot(inputs[step], turned, preferred_element_type=F32)
 
         def part(block, p):
             at = ROW * (p - begin)
@@ -365,7 +362,7 @@
         ),
         in_specs=[vmem()],
         out_specs=(vmem(),) * 4,
-        compiler_params=pltpu.CompilerParams(vmem_limit_bytes=VMEM_LIMIT),
+        compiler_params=pltpu.CompilerParams(vmem_limit_bytes=8 * MIB),
         name="weave",
     )(weights)
 
@@ -388,7 +385,7 @@
             pltpu.VMEM((2, seen, 2 * C, ROW), BF16),
             pltpu.VMEM((STEPS // 2, FEATS + C, LANES), F32),
         ],
-        compiler_params=pltpu.CompilerParams(vmem_limit_bytes=VMEM_LIMIT),
+        compiler_params=pltpu.CompilerParams(vmem_limit_bytes=40 * MIB),
         name="rollout",
     )(received, *woven)
 
@@ -418,7 +415,7 @@
         ),
         in_specs=[vmem()],
         out_specs=(vmem(),) * 3,
-        compiler_params=pltpu.CompilerParams(vmem_limit_bytes=VMEM_LIMIT),
+        compiler_params=pltpu.CompilerParams(vmem_limit_bytes=4 * MIB),
         name="finish",
     )(parts)
 

time: 78.3 us -> 73.6 us (0.940)
  Pallas kernels: 23.9 us -> 19.4 us
  waiting for transfers between devices: 5.17 us -> 7.5 us
  local copies, waits for them, and re-layouts: 2.48 us -> 0.95 us
  other arithmetic: 1.19 us -> 0.31 us
    all_to_all x1, waiting for transfers between devices: 3.17 us -> 5.72 us  [body(): received = lax.all_to_all(windows, 'gx', 0, 0, tiled=True)]
    pallas_call x1, Pallas kernels: 3.31 us -> 1.48 us  [weave(): pl.pallas_call(weave_kernel, out_shape=(jax.ShapeDtypeStruct((STEPS, 2 *...]
    pallas_call x1, Pallas kernels: 17 us -> 15.2 us  [rollout(): pl.pallas_call(rollout_kernel, out_shape=(jax.ShapeDtypeStruct((STEPS //...]
    pallas_call x1, Pallas kernels: 1.71 us -> 0.75 us  [finish(): pl.pallas_call(finish_kernel, out_shape=(jax.ShapeDtypeStruct((depth, 7 *...]
    convert_element_type x1, other arithmetic: 0.9 us -> 0.01 us  [everyones(): block.astype(BF16)[None]]
    unnamed x8 -> x6, local copies, waits for them, and re-layouts: 1.35 us -> 0.56 us
  transfers between devices with their start and end apart: 3 -> 3, of which waited for: 3 -> 3; matrix products, arithmetic and copies ran while one was open for 2% -> 1% of each run, Pallas kernels for 4% -> 2%
where the time goes in v4:
time: 73.6 us; the launch traced here: 73.3 us
  blocking collectives  36.6 us (50%)
  Pallas kernels  19.4 us (26%)
  starting transfers between devices  7.71 us (10%)
  waiting for transfers between devices  7.5 us (10%)
  local copies, waits for them, and re-layouts  0.95 us (1%)
  between operations  0.75 us (1%)
    all_to_all x2, blocking collectives, everyones(): return lax.all_to_all(same, axis, 0, 0, tiled=True)  36.6 us
    pallas_call x1, Pallas kernels, rollout(): pl.pallas_call(rollout_kernel, out_shape=(jax.ShapeDtypeStruct((STEPS //...  15.2 us
    all_to_all x1, starting transfers between devices, body(): received = lax.all_to_all(windows, 'gx', 0, 0, tiled=True)  7.52 us
    all_to_all x1, waiting for transfers between devices, body(): received = lax.all_to_all(windows, 'gx', 0, 0, tiled=True)  5.72 us
    pallas_call x1, Pallas kernels, prepare(): pl.pallas_call(prepare_kernel, out_shape=jax.ShapeDtypeStruct((SLABS, CHU...  1.96 us
    ppermute x2, waiting for transfers between devices, swap(): lax.ppermute(block, axis, [(i, i ^ distance) for i in range(devices)])  1.78 us
    pallas_call x1, Pallas kernels, weave(): pl.pallas_call(weave_kernel, out_shape=(jax.ShapeDtypeStruct((STEPS, 2 *...  1.48 us
  transfers between devices with their start and end apart: 3, of which 3 were waited for; matrix products, arithmetic and copies ran while one was open for 1% of the time, Pallas kernels for 2%

profile of v4, /device:TPU:8, one launch (start us, length us, event | category | flops | bytes accessed | tf_op | source)
XLA Modules:
  0.0 73.3 jit_solution(14725842068920753214)
XLA Ops:
  0.6 2.0 %prepare.1 = bf16[16,64,256]{2,1,0:T(8,128)(2,1)} custom-call(s32[2]{0:T(128)} %order.1, f32[2,256,128]{2,1,0:T(8,128)} %bitcast.10, f32[2,256,128]{2,1,0:T(8,128)} %bitcast.11), custom_call_target="tpu_custom_call" | custom-call | tf_op jit(solution)/shard_map/prepare/pallas_call | solution.py:344
  2.6 0.0 copy-start.1
  2.6 0.0 copy-start
  2.6 7.5 %all-to-all-start = ((bf16[16,64,256]{2,1,0:T(8,128)(2,1)}), bf16[16,64,256]{2,1,0:T(8,128)(2,1)S(1)}, u32[]{:S(2)}, u32[]{:S(2)}) async-start(bf16[16,64,256]{2,1,0:T(8,128)(2,1)} %prepare.1), calls=%async_computation | async-start | bytes 1048576 | tf_op jit(solution)/shard_map/all_to_all | solution.py:462
  10.1 0.0 copy-done.1
  10.1 0.0 copy-done
  10.2 0.1 copy.26
  10.3 0.0 copy-start.2
  10.3 0.1 collective-permute-start
  10.4 0.6 copy-done.2
  11.0 0.1 copy.27
  11.1 0.5 collective-permute-done
  11.7 0.1 maximum_add_fusion
  11.9 1.5 %weave.1 = (bf16[8,144,128]{2,1,0:T(8,128)(2,1)S(1)}, bf16[8,16,128]{2,1,0:T(8,128)(2,1)S(1)}, bf16[8,128,16]{2,1,0:T(8,128)(2,1)S(1)}, bf16[8,112,144]{2,1,0:T(8,128)(2,1)S(1)}) custom-call(f32[8,80,64]{2,1,0:T(8,128)S(1)} %pad.15.weights), custom_call_target="tpu_custom_call" | custom-call | tf_op jit(solution)/shard_map/weave/pallas_call | solution.py:355
  13.4 5.7 %all-to-all-done.received = bf16[16,64,256]{2,1,0:T(8,128)(2,1)S(1)} async-done(((bf16[16,64,256]{2,1,0:T(8,128)(2,1)}), bf16[16,64,256]{2,1,0:T(8,128)(2,1)S(1)}, u32[]{:S(2)}, u32[]{:S(2)}) %all-to-all-start) | async-done | bytes 524320 | tf_op jit(solution)/shard_map/all_to_all | solution.py:462
  19.1 15.2 %rollout.1 = (f32[2,72,128]{2,1,0:T(8,128)S(1)}, f32[2,72,128]{2,1,0:T(8,128)S(1)}) custom-call(bf16[16,64,256]{2,1,0:T(8,128)(2,1)S(1)} %all-to-all-done.received, bf16[8,144,128]{2,1,0:T(8,128)(2,1)S(1)} %get-tuple-element.20.first, bf16[8,16,128]{2,1,0:T(8,128)(2,1)S(1)} %get-tuple-element.21.second, ...), custom_call_target="tpu_custom_call" | custom-call | tf_op jit(solution)/shard_map/rollout/pallas_call | solution.py:373
  34.3 0.1 collective-permute-start.1
  34.4 1.3 %collective-permute-done.1 = f32[2,72,128]{2,1,0:T(8,128)S(1)} collective-permute-done((f32[2,72,128]{2,1,0:T(8,128)S(1)}, f32[2,72,128]{2,1,0:T(8,128)S(1)}, u32[]{:S(2)}, u32[]{:S(2)}) %collective-permute-start.1) | collective-permute-done | bytes 73760 | tf_op jit(solution)/shard_map/ppermute | solution.py:425
  35.7 0.1 broadcast_in_dim.4
  35.7 16.7 %all_to_all.15 = bf16[16,144,128]{2,1,0:T(8,128)(2,1)S(1)} all-to-all(bf16[16,144,128]{2,1,0:T(8,128)(2,1)S(1)} %broadcast_in_dim.4), channel_id=1, replica_groups=mesh['section'=2,'gx'=16,'dp'=8] {'gx'}, dimensions={0} | all-to-all | bytes 1179648 | tf_op jit(solution)/shard_map/all_to_all | solution.py:430
  52.4 0.1 reduce_sum.12
  52.6 19.9 %all_to_all.16.parts = bf16[8,144,128]{2,1,0:T(8,128)(2,1)S(1)} all-to-all(bf16[8,144,128]{2,1,0:T(8,128)(2,1)S(1)} %broadcast_in_dim.5), channel_id=1, replica_groups=mesh['section'=2,'gx'=16,'dp'=8] {'dp'}, dimensions={0} | all-to-all | bytes 589824 | tf_op jit(solution)/shard_map/all_to_all | solution.py:430
  72.5 0.8 %finish.1 = (f32[4,56,64]{2,1,0:T(8,128)}, f32[4,64]{1,0:T(4,128)}, f32[4,8,64]{2,1,0:T(8,128)}) custom-call(bf16[8,144,128]{2,1,0:T(8,128)(2,1)S(1)} %all_to_all.16.parts), custom_call_target="tpu_custom_call" | custom-call | tf_op jit(solution)/shard_map/finish/pallas_call | solution.py:409
  (9 shorter events, 0.2 us)
Async XLA Ops:
  2.6 7.5 %copy-start.1 = (f32[4,8,64]{2,1,0:T(8,128)S(1)}, f32[4,8,64]{2,1,0:T(8,128)}, u32[]{:S(2)}) copy-start(f32[4,8,64]{2,1,0:T(8,128)} %param.10) | copy-start | bytes 24580
  2.6 7.5 %copy-start = (f32[4,64,56]{1,2,0:T(8,128)S(1)}, f32[4,64,56]{1,2,0:T(8,128)}, u32[]{:S(2)}) copy-start(f32[4,64,56]{1,2,0:T(8,128)} %param.8) | copy-start | bytes 172036
  2.6 16.5 %all-to-all-start = ((bf16[16,64,256]{2,1,0:T(8,128)(2,1)}), bf16[16,64,256]{2,1,0:T(8,128)(2,1)S(1)}, u32[]{:S(2)}, u32[]{:S(2)}) async-start(bf16[16,64,256]{2,1,0:T(8,128)(2,1)} %prepare.1), calls=%async_computation | async-start | bytes 1048576 | tf_op jit(solution)/shard_map/all_to_all | solution.py:462
  10.3 0.7 copy-start.2
  10.3 1.4 %collective-permute-start = (bf16[4,72,64]{2,1,0:T(8,128)(2,1)S(1)}, bf16[4,72,64]{2,1,0:T(8,128)(2,1)S(1)}, u32[]{:S(2)}, u32[]{:S(2)}) collective-permute-start(bf16[4,72,64]{2,1,0:T(8,128)(2,1)S(1)} %fusion.1), channel_id=1, source_target_pairs={{0,128},{128,0},{1,129},{129,1},{2,130},{130,2},{3,131},{131,3},{4... | collective-permute-start | bytes 110600 | tf_op jit(solution)/shard_map/ppermute | solution.py:425
  34.3 1.3 %collective-permute-start.1 = (f32[2,72,128]{2,1,0:T(8,128)S(1)}, f32[2,72,128]{2,1,0:T(8,128)S(1)}, u32[]{:S(2)}, u32[]{:S(2)}) collective-permute-start(f32[2,72,128]{2,1,0:T(8,128)S(1)} %get-tuple-element.25), channel_id=1, source_target_pairs={{0,128},{128,0},{1,129},{129,1},{2,130},{130,2},{3,131},{131,3},{4... | collective-permute-start | bytes 221192 | tf_op jit(solution)/shard_map/ppermute | solution.py:425

commit v5 on v4

--- a/solution.py
+++ b/solution.py
@@ -34,6 +34,7 @@
 OWN_AT = 16
 TWIN = 24
 CHUNK = WIN + TWIN
+SENT = 4
 SLAB_CELLS = 32
 PAIRS = WIN // 2
 SEEN = 9
@@ -43,18 +44,34 @@
 VMEM_LIMIT = 56 * MIB
 
 
-def prepare_kernel(order, fields, targets, out):
+def prepare_kernel(order, fields, targets, out, field_here, target_here, windows, done):
     member = lax.axis_index("section")
-    field = fields[member].T
-    target = targets[order[member]].T
+    field_copy = pltpu.make_async_copy(fields.at[member], field_here, done.at[0])
+    target_copy = pltpu.make_async_copy(targets.at[order[member]], target_here, done.at[1])
+    field_copy.start()
+    target_copy.start()
+    field_copy.wait()
+    field = field_here[...].T
+    target_copy.wait()
+    target = target_here[...].T
     field = jnp.concatenate([field[NZ - OWN_AT :], field, field[: WIN - OWN_AT]], axis=0)
     target = jnp.concatenate([target[NZ - OWN :], target, target[: TWIN - OWN]], axis=0)
+    sent = []
     for slab in range(SLABS):
         begin = slab * OWN
         both = jnp.concatenate(
             [field[begin : begin + WIN], target[begin : begin + TWIN]], axis=0
         )
-        out[slab] = both.astype(BF16)
+        windows[slab] = both.astype(BF16)
+        if slab % SENT == SENT - 1:
+            some = pl.ds(slab + 1 - SENT, SENT)
+            copy = pltpu.make_async_copy(
+                windows.at[some], out.at[some], done.at[2 + slab // SENT]
+            )
+            copy.start()
+            sent.append(copy)
+    for copy in sent:
+        copy.wait()
 
 
 def roll_lanes(tile, shift):
@@ -332,20 +349,31 @@
         backward_step(step, PAIRS - OWN // 2 - step)
 
     half = STEPS // 4
-    mine[...] = grads[pl.ds(section * half, half)]
-    yours[...] = grads[pl.ds((1 - section) * half, half)]
+    mine[...] = grads[pl.ds(section * half, half)].reshape(mine.shape)
+    theirs = grads[pl.ds((1 - section) * half, half)]
+    yours[...] = theirs.reshape(yours.shape).astype(BF16)
 
 
 def vmem():
     return pl.BlockSpec(memory_space=pltpu.VMEM)
+
+
+def hbm():
+    return pl.BlockSpec(memory_space=pl.ANY)
 
 
 def prepare(order, fields, targets):
     return pl.pallas_call(
         prepare_kernel,
         out_shape=jax.ShapeDtypeStruct((SLABS, CHUNK, C * SLAB_CELLS), BF16),
-        in_specs=[pl.BlockSpec(memory_space=pltpu.SMEM), vmem(), vmem()],
-        out_specs=vmem(),
+        in_specs=[pl.BlockSpec(memory_space=pltpu.SMEM), hbm(), hbm()],
+        out_specs=hbm(),
+        scratch_shapes=[
+            pltpu.VMEM(fields.shape[1:], F32),
+            pltpu.VMEM(targets.shape[1:], F32),
+            pltpu.VMEM((SLABS, CHUNK, C * SLAB_CELLS), BF16),
+            pltpu.SemaphoreType.DMA((2 + SLABS // SENT,)),
+        ],
         compiler_params=pltpu.CompilerParams(vmem_limit_bytes=VMEM_LIMIT),
         name="prepare",
     )(order, fields, targets)
@@ -372,7 +400,10 @@
     seen = PAIRS - SEEN
     return pl.pallas_call(
         rollout_kernel,
-        out_shape=(jax.ShapeDtypeStruct((STEPS // 4, FEATS + C, LANES), F32),) * 2,
+        out_shape=(
+            jax.ShapeDtypeStruct((STEPS // 4 * (FEATS + C), LANES), F32),
+            jax.ShapeDtypeStruct((STEPS // 4 * (FEATS + C), LANES), BF16),
+        ),
         in_specs=[vmem()] * 5,
         out_specs=(vmem(),) * 2,
         scratch_shapes=[
@@ -461,8 +492,7 @@
     weights = all_weights(weight_in, bias_in, weight_out, section)
     received = lax.all_to_all(windows, "gx", 0, 0, tiled=True)
     mine, yours = rollout(received, weave(weights))
-    total = mine + swap(yours, "section", 1)
-    total = total.reshape(-1, LANES)
+    total = mine + swap(yours, "section", 1).astype(F32)
     total = jnp.sum(everyones(total, "gx").astype(F32), axis=0)
     grad_in, grad_bias, grad_out = finish(everyones(total, "dp"), depth)
     return (grad_in.transpose(0, 2, 1), grad_bias, grad_out)

time: 73.6 us -> 74.2 us (level)
  no operation moved by 1% of the time
where the time goes in v5:
time: 74.2 us; the launch traced here: 73.9 us
  blocking collectives  36.6 us (49%)
  Pallas kernels  20.1 us (27%)
  starting transfers between devices  7.72 us (10%)
  waiting for transfers between devices  7.45 us (10%)
  local copies, waits for them, and re-layouts  0.96 us (1%)
  between operations  0.78 us (1%)
    all_to_all x2, blocking collectives, everyones(): return lax.all_to_all(same, axis, 0, 0, tiled=True)  36.6 us
    pallas_call x1, Pallas kernels, rollout(): pl.pallas_call(rollout_kernel, out_shape=(jax.ShapeDtypeStruct((STEPS //...  15.2 us
    all_to_all x1, starting transfers between devices, body(): received = lax.all_to_all(windows, 'gx', 0, 0, tiled=True)  7.54 us
    all_to_all x1, waiting for transfers between devices, body(): received = lax.all_to_all(windows, 'gx', 0, 0, tiled=True)  5.72 us
    pallas_call x1, Pallas kernels, prepare(): pl.pallas_call(prepare_kernel, out_shape=jax.ShapeDtypeStruct((SLABS, CHU...  2.63 us
    ppermute x2, waiting for transfers between devices, swap(): lax.ppermute(block, axis, [(i, i ^ distance) for i in range(devices)])  1.72 us
  transfers between devices with their start and end apart: 3, of which 3 were waited for; matrix products, arithmetic and copies ran while one was open for 1% of the time, Pallas kernels for 2%

profile of v5, /device:TPU:8, one launch (start us, length us, event | category | flops | bytes accessed | tf_op | source)
XLA Modules:
  0.0 73.9 jit_solution(2532997776490307332)
XLA Ops:
  0.6 2.6 %prepare.1 = bf16[16,64,256]{2,1,0:T(8,128)(2,1)} custom-call(s32[2]{0:T(128)} %order.1, f32[2,256,128]{2,1,0:T(8,128)} %bitcast.9, f32[2,256,128]{2,1,0:T(8,128)} %bitcast.10), custom_call_target="tpu_custom_call" | custom-call | tf_op jit(solution)/shard_map/prepare/pallas_call | solution.py:366
  3.3 0.0 copy-start.1
  3.3 0.0 copy-start
  3.3 7.5 %all-to-all-start = ((bf16[16,64,256]{2,1,0:T(8,128)(2,1)}), bf16[16,64,256]{2,1,0:T(8,128)(2,1)S(1)}, u32[]{:S(2)}, u32[]{:S(2)}) async-start(bf16[16,64,256]{2,1,0:T(8,128)(2,1)} %prepare.1), calls=%async_computation | async-start | bytes 1048576 | tf_op jit(solution)/shard_map/all_to_all | solution.py:493
  10.8 0.0 copy-done.1
  10.8 0.0 copy-done
  10.9 0.1 copy.26
  11.0 0.0 copy-start.2
  11.0 0.1 collective-permute-start
  11.1 0.6 copy-done.2
  11.7 0.1 copy.27
  11.9 0.5 collective-permute-done
  12.4 0.1 maximum_add_fusion
  12.6 1.5 %weave.1 = (bf16[8,144,128]{2,1,0:T(8,128)(2,1)S(1)}, bf16[8,16,128]{2,1,0:T(8,128)(2,1)S(1)}, bf16[8,128,16]{2,1,0:T(8,128)(2,1)S(1)}, bf16[8,112,144]{2,1,0:T(8,128)(2,1)S(1)}) custom-call(f32[8,80,64]{2,1,0:T(8,128)S(1)} %pad.15.weights), custom_call_target="tpu_custom_call" | custom-call | tf_op jit(solution)/shard_map/weave/pallas_call | solution.py:383
  14.1 5.7 %all-to-all-done.received = bf16[16,64,256]{2,1,0:T(8,128)(2,1)S(1)} async-done(((bf16[16,64,256]{2,1,0:T(8,128)(2,1)}), bf16[16,64,256]{2,1,0:T(8,128)(2,1)S(1)}, u32[]{:S(2)}, u32[]{:S(2)}) %all-to-all-start) | async-done | bytes 524320 | tf_op jit(solution)/shard_map/all_to_all | solution.py:493
  19.8 15.2 %rollout.1 = (f32[144,128]{1,0:T(8,128)S(1)}, bf16[144,128]{1,0:T(8,128)(2,1)S(1)}) custom-call(bf16[16,64,256]{2,1,0:T(8,128)(2,1)S(1)} %all-to-all-done.received, bf16[8,144,128]{2,1,0:T(8,128)(2,1)S(1)} %get-tuple-element.20.first, bf16[8,16,128]{2,1,0:T(8,128)(2,1)S(1)} %get-tuple-element.21.second, ...), custom_call_target="tpu_custom_call" | custom-call | tf_op jit(solution)/shard_map/rollout/pallas_call | solution.py:401
  35.0 0.1 collective-permute-start.1
  35.1 1.2 %collective-permute-done.1 = bf16[144,128]{1,0:T(8,128)(2,1)S(1)} collective-permute-done((bf16[144,128]{1,0:T(8,128)(2,1)S(1)}, bf16[144,128]{1,0:T(8,128)(2,1)S(1)}, u32[]{:S(2)}, u32[]{:S(2)}) %collective-permute-start.1) | collective-permute-done | bytes 36896 | tf_op jit(solution)/shard_map/ppermute | solution.py:456
  36.3 0.1 broadcast_in_dim.4
  36.4 16.7 %all_to_all.15 = bf16[16,144,128]{2,1,0:T(8,128)(2,1)S(1)} all-to-all(bf16[16,144,128]{2,1,0:T(8,128)(2,1)S(1)} %broadcast_in_dim.4), channel_id=1, replica_groups=mesh['section'=2,'gx'=16,'dp'=8] {'gx'}, dimensions={0} | all-to-all | bytes 1179648 | tf_op jit(solution)/shard_map/all_to_all | solution.py:461
  53.1 0.1 reduce_sum.12
  53.2 19.9 %all_to_all.16.parts = bf16[8,144,128]{2,1,0:T(8,128)(2,1)S(1)} all-to-all(bf16[8,144,128]{2,1,0:T(8,128)(2,1)S(1)} %broadcast_in_dim.5), channel_id=1, replica_groups=mesh['section'=2,'gx'=16,'dp'=8] {'dp'}, dimensions={0} | all-to-all | bytes 589824 | tf_op jit(solution)/shard_map/all_to_all | solution.py:461
  73.2 0.8 %finish.1 = (f32[4,56,64]{2,1,0:T(8,128)}, f32[4,64]{1,0:T(4,128)}, f32[4,8,64]{2,1,0:T(8,128)}) custom-call(bf16[8,144,128]{2,1,0:T(8,128)(2,1)S(1)} %all_to_all.16.parts), custom_call_target="tpu_custom_call" | custom-call | tf_op jit(solution)/shard_map/finish/pallas_call | solution.py:440
  (9 shorter events, 0.2 us)
Async XLA Ops:
  3.3 7.6 %copy-start.1 = (f32[4,8,64]{2,1,0:T(8,128)S(1)}, f32[4,8,64]{2,1,0:T(8,128)}, u32[]{:S(2)}) copy-start(f32[4,8,64]{2,1,0:T(8,128)} %param.10) | copy-start | bytes 24580
  3.3 7.6 %copy-start = (f32[4,64,56]{1,2,0:T(8,128)S(1)}, f32[4,64,56]{1,2,0:T(8,128)}, u32[]{:S(2)}) copy-start(f32[4,64,56]{1,2,0:T(8,128)} %param.8) | copy-start | bytes 172036
  3.3 16.5 %all-to-all-start = ((bf16[16,64,256]{2,1,0:T(8,128)(2,1)}), bf16[16,64,256]{2,1,0:T(8,128)(2,1)S(1)}, u32[]{:S(2)}, u32[]{:S(2)}) async-start(bf16[16,64,256]{2,1,0:T(8,128)(2,1)} %prepare.1), calls=%async_computation | async-start | bytes 1048576 | tf_op jit(solution)/shard_map/all_to_all | solution.py:493
  11.0 0.7 copy-start.2
  11.0 1.4 %collective-permute-start = (bf16[4,72,64]{2,1,0:T(8,128)(2,1)S(1)}, bf16[4,72,64]{2,1,0:T(8,128)(2,1)S(1)}, u32[]{:S(2)}, u32[]{:S(2)}) collective-permute-start(bf16[4,72,64]{2,1,0:T(8,128)(2,1)S(1)} %fusion.1), channel_id=1, source_target_pairs={{0,128},{128,0},{1,129},{129,1},{2,130},{130,2},{3,131},{131,3},{4... | collective-permute-start | bytes 110600 | tf_op jit(solution)/shard_map/ppermute | solution.py:456
  35.0 1.3 %collective-permute-start.1 = (bf16[144,128]{1,0:T(8,128)(2,1)S(1)}, bf16[144,128]{1,0:T(8,128)(2,1)S(1)}, u32[]{:S(2)}, u32[]{:S(2)}) collective-permute-start(bf16[144,128]{1,0:T(8,128)(2,1)S(1)} %get-tuple-element.25), channel_id=1, source_target_pairs={{0,128},{128,0},{1,129},{129,1},{2,130},{130,2},{3,131},{131,3},{4... | collective-permute-start | bytes 110600 | tf_op jit(solution)/shard_map/ppermute | solution.py:456

commit v6 on v4

--- a/solution.py
+++ b/solution.py
@@ -34,6 +34,8 @@
 OWN_AT = 16
 TWIN = 24
 CHUNK = WIN + TWIN
+PAIRED = STEPS // 4
+KEPT = 7 * C + C
 SLAB_CELLS = 32
 PAIRS = WIN // 2
 SEEN = 9
@@ -169,7 +171,7 @@
 
 def rollout_kernel(
     received, first, second, second_back, first_back, mine, yours,
-    unpack, state, last, target, slopes, inputs, cots, grads,
+    unpack, state, last, target, slopes, inputs, cots, grads, outer,
 ):
     section = lax.axis_index("section")
     shifts = Shifts()
@@ -279,9 +281,10 @@
         rows = []
         for block in range(FEATS // C):
             at = 2 * H + 2 * C * block
-            rows.append(grad[at : at + C, : 2 * H] + roll_lanes(grad[at + C : at + 2 * C, : 2 * H], -H))
+            upper = roll_lanes(grad[at + C : at + 2 * C, : 2 * H], -H)
+            rows.append(grad[at : at + C, : 2 * H] + upper)
         hidden = grad[: 2 * H, 2 * H :].T
-        rows.append(hidden[:C] + roll_lanes(hidden[C:], -H))
+        rows.insert(7, hidden[:C] + roll_lanes(hidden[C:], -H))
         return jnp.concatenate(rows, axis=0)
 
     def backward_step(step, begin):
@@ -293,8 +296,7 @@
         cot_pre = cot_hidden.astype(BF16) * slope
         both = jnp.concatenate([cot_pre, cot], axis=0)
         spread = jnp.dot(first_back[step], both, preferred_element_type=F32)
-        turned = both[:, ROW * (count - OWN // 2) :].astype(F32).T.astype(BF16)
-        grad = jnp.dot(inputs[step], turned, preferred_element_type=F32)
+        outer[step] = both[:, ROW * (count - OWN // 2) :]
 
         def part(block, p):
             at = ROW * (p - begin)
@@ -322,18 +324,26 @@
             total = jnp.concatenate([low, high], axis=0)
             cots[then, p - SEEN] = (CORRECTION_GAIN * total).astype(BF16)
 
+
+    for step in reversed(range(STEPS)):
+        backward_step(step, PAIRS - OWN // 2 - step)
+
+    for step in reversed(range(STEPS)):
+        grad = lax.dot_general(
+            inputs[step], outer[step], (((1,), (1,)), ((), ())), preferred_element_type=F32
+        )
         summed = gather_grads(grad)
         if step % 2 == 1:
             grads[step // 2] = roll_lanes(summed, H)
         else:
             grads[step // 2] = jnp.where(left_half, summed, grads[step // 2])
 
-    for step in reversed(range(STEPS)):
-        backward_step(step, PAIRS - OWN // 2 - step)
-
-    half = STEPS // 4
-    mine[...] = grads[pl.ds(section * half, half)]
-    yours[...] = grads[pl.ds((1 - section) * half, half)]
+    first_row = lax.broadcasted_iota(jnp.int32, (C, LANES), 0) == 0
+    for out, which in ((mine, section), (yours, 1 - section)):
+        sides = grads[pl.ds(which * PAIRED, PAIRED)]
+        for pair in range(PAIRED):
+            out[pl.ds(pair * KEPT, KEPT), :] = sides[pair, :KEPT]
+        out[pl.ds(PAIRED * KEPT, C), :] = jnp.where(first_row, sides[0, KEPT:], sides[1, KEPT:])
 
 
 def vmem():
@@ -372,7 +382,7 @@
     seen = PAIRS - SEEN
     return pl.pallas_call(
         rollout_kernel,
-        out_shape=(jax.ShapeDtypeStruct((STEPS // 4, FEATS + C, LANES), F32),) * 2,
+        out_shape=(jax.ShapeDtypeStruct((PAIRED * KEPT + C, LANES), F32),) * 2,
         in_specs=[vmem()] * 5,
         out_specs=(vmem(),) * 2,
         scratch_shapes=[
@@ -384,6 +394,7 @@
             pltpu.VMEM((STEPS, 2 * H + 2 * FEATS, own), BF16),
             pltpu.VMEM((2, seen, 2 * C, ROW), BF16),
             pltpu.VMEM((STEPS // 2, FEATS + C, LANES), F32),
+            pltpu.VMEM((STEPS, 2 * H + 2 * C, own), BF16),
         ],
         compiler_params=pltpu.CompilerParams(vmem_limit_bytes=40 * MIB),
         name="rollout",
@@ -394,15 +405,15 @@
     total = parts[0].astype(F32)
     for i in range(1, parts.shape[0]):
         total = total + parts[i].astype(F32)
-    rows = FEATS + C
+    biases = total[PAIRED * KEPT :]
     for step in range(grad_in.shape[0]):
-        at = step // 2 * rows
-        side = total[at : at + rows]
+        pair = step // 2
+        side, bias = total[pair * KEPT : (pair + 1) * KEPT], biases
         if step % 2:
-            side = roll_lanes(side, H)
+            side, bias = roll_lanes(side, H), roll_lanes(bias, H)
         grad_in[step] = side[: 7 * C, :H]
-        grad_bias[pl.ds(step, 1), :] = side[7 * C : 7 * C + 1, :H]
-        grad_out[step] = side[FEATS:, :H]
+        grad_out[step] = side[7 * C :, :H]
+        grad_bias[pl.ds(step, 1), :] = bias[pair : pair + 1, :H]
 
 
 def finish(parts, depth):
@@ -462,7 +473,6 @@
     received = lax.all_to_all(windows, "gx", 0, 0, tiled=True)
     mine, yours = rollout(received, weave(weights))
     total = mine + swap(yours, "section", 1)
-    total = total.reshape(-1, LANES)
     total = jnp.sum(everyones(total, "gx").astype(F32), axis=0)
     grad_in, grad_bias, grad_out = finish(everyones(total, "dp"), depth)
     return (grad_in.transpose(0, 2, 1), grad_bias, grad_out)

time: 73.6 us -> 72.5 us (0.985)
  no operation moved by 1% of the time
where the time goes in v6:
time: 72.5 us; the launch traced here: 72.1 us
  blocking collectives  35.9 us (50%)
  Pallas kernels  19 us (26%)
  starting transfers between devices  7.71 us (11%)
  waiting for transfers between devices  7.49 us (10%)
  local copies, waits for them, and re-layouts  0.95 us (1%)
  between operations  0.76 us (1%)
    all_to_all x2, blocking collectives, everyones(): return lax.all_to_all(same, axis, 0, 0, tiled=True)  35.9 us
    pallas_call x1, Pallas kernels, rollout(): pl.pallas_call(rollout_kernel, out_shape=(jax.ShapeDtypeStruct((PAIRED *...  14.8 us
    all_to_all x1, starting transfers between devices, body(): received = lax.all_to_all(windows, 'gx', 0, 0, tiled=True)  7.52 us
    all_to_all x1, waiting for transfers between devices, body(): received = lax.all_to_all(windows, 'gx', 0, 0, tiled=True)  5.72 us
    pallas_call x1, Pallas kernels, prepare(): pl.pallas_call(prepare_kernel, out_shape=jax.ShapeDtypeStruct((SLABS, CHU...  1.96 us
    ppermute x2, waiting for transfers between devices, swap(): lax.ppermute(block, axis, [(i, i ^ distance) for i in range(devices)])  1.77 us
    pallas_call x1, Pallas kernels, weave(): pl.pallas_call(weave_kernel, out_shape=(jax.ShapeDtypeStruct((STEPS, 2 *...  1.48 us
  transfers between devices with their start and end apart: 3, of which 3 were waited for; matrix products, arithmetic and copies ran while one was open for 1% of the time, Pallas kernels for 2%

profile of v6, /device:TPU:8, one launch (start us, length us, event | category | flops | bytes accessed | tf_op | source)
XLA Modules:
  0.0 72.1 jit_solution(16553675328475651180)
XLA Ops:
  0.6 2.0 %prepare.1 = bf16[16,64,256]{2,1,0:T(8,128)(2,1)} custom-call(s32[2]{0:T(128)} %order.1, f32[2,256,128]{2,1,0:T(8,128)} %bitcast.9, f32[2,256,128]{2,1,0:T(8,128)} %bitcast.10), custom_call_target="tpu_custom_call" | custom-call | tf_op jit(solution)/shard_map/prepare/pallas_call | solution.py:354
  2.6 0.0 copy-start.1
  2.6 0.0 copy-start
  2.6 7.5 %all-to-all-start = ((bf16[16,64,256]{2,1,0:T(8,128)(2,1)}), bf16[16,64,256]{2,1,0:T(8,128)(2,1)S(1)}, u32[]{:S(2)}, u32[]{:S(2)}) async-start(bf16[16,64,256]{2,1,0:T(8,128)(2,1)} %prepare.1), calls=%async_computation | async-start | bytes 1048576 | tf_op jit(solution)/shard_map/all_to_all | solution.py:473
  10.1 0.0 copy-done.1
  10.1 0.0 copy-done
  10.2 0.1 copy.26
  10.3 0.0 copy-start.2
  10.3 0.1 collective-permute-start
  10.4 0.6 copy-done.2
  11.0 0.1 copy.27
  11.1 0.5 collective-permute-done
  11.7 0.1 maximum_add_fusion
  11.9 1.5 %weave.1 = (bf16[8,144,128]{2,1,0:T(8,128)(2,1)S(1)}, bf16[8,16,128]{2,1,0:T(8,128)(2,1)S(1)}, bf16[8,128,16]{2,1,0:T(8,128)(2,1)S(1)}, bf16[8,112,144]{2,1,0:T(8,128)(2,1)S(1)}) custom-call(f32[8,80,64]{2,1,0:T(8,128)S(1)} %pad.15.weights), custom_call_target="tpu_custom_call" | custom-call | tf_op jit(solution)/shard_map/weave/pallas_call | solution.py:365
  13.4 5.7 %all-to-all-done.received = bf16[16,64,256]{2,1,0:T(8,128)(2,1)S(1)} async-done(((bf16[16,64,256]{2,1,0:T(8,128)(2,1)}), bf16[16,64,256]{2,1,0:T(8,128)(2,1)S(1)}, u32[]{:S(2)}, u32[]{:S(2)}) %all-to-all-start) | async-done | bytes 524320 | tf_op jit(solution)/shard_map/all_to_all | solution.py:473
  19.1 14.8 %rollout.1 = (f32[136,128]{1,0:T(8,128)S(1)}, f32[136,128]{1,0:T(8,128)S(1)}) custom-call(bf16[16,64,256]{2,1,0:T(8,128)(2,1)S(1)} %all-to-all-done.received, bf16[8,144,128]{2,1,0:T(8,128)(2,1)S(1)} %get-tuple-element.20.first, bf16[8,16,128]{2,1,0:T(8,128)(2,1)S(1)} %get-tuple-element.21.second, bf16[8,128,16]{2,1,0:T(8,128)(2,1)S(1)} %get-tuple-element.22.second_back, ...), custom_call_target="tpu_custom_call" | custom-call | tf_op jit(solution)/shard_map/rollout/pallas_call | solution.py:383
  33.9 0.1 collective-permute-start.1
  34.0 1.2 %collective-permute-done.1 = f32[136,128]{1,0:T(8,128)S(1)} collective-permute-done((f32[136,128]{1,0:T(8,128)S(1)}, f32[136,128]{1,0:T(8,128)S(1)}, u32[]{:S(2)}, u32[]{:S(2)}) %collective-permute-start.1) | collective-permute-done | bytes 69664 | tf_op jit(solution)/shard_map/ppermute | solution.py:436
  35.2 0.1 broadcast_in_dim.4
  35.3 16.5 %all_to_all.15 = bf16[16,136,128]{2,1,0:T(8,128)(2,1)S(1)} all-to-all(bf16[16,136,128]{2,1,0:T(8,128)(2,1)S(1)} %broadcast_in_dim.4), channel_id=1, replica_groups=mesh['section'=2,'gx'=16,'dp'=8] {'gx'}, dimensions={0} | all-to-all | bytes 1114112 | tf_op jit(solution)/shard_map/all_to_all | solution.py:441
  51.8 0.1 reduce_sum.12
  52.0 19.4 %all_to_all.16.parts = bf16[8,136,128]{2,1,0:T(8,128)(2,1)S(1)} all-to-all(bf16[8,136,128]{2,1,0:T(8,128)(2,1)S(1)} %broadcast_in_dim.5), channel_id=1, replica_groups=mesh['section'=2,'gx'=16,'dp'=8] {'dp'}, dimensions={0} | all-to-all | bytes 557056 | tf_op jit(solution)/shard_map/all_to_all | solution.py:441
  71.4 0.8 %finish.1 = (f32[4,56,64]{2,1,0:T(8,128)}, f32[4,64]{1,0:T(4,128)}, f32[4,8,64]{2,1,0:T(8,128)}) custom-call(bf16[8,136,128]{2,1,0:T(8,128)(2,1)S(1)} %all_to_all.16.parts), custom_call_target="tpu_custom_call" | custom-call | tf_op jit(solution)/shard_map/finish/pallas_call | solution.py:420
  (9 shorter events, 0.1 us)
Async XLA Ops:
  2.6 7.5 %copy-start.1 = (f32[4,8,64]{2,1,0:T(8,128)S(1)}, f32[4,8,64]{2,1,0:T(8,128)}, u32[]{:S(2)}) copy-start(f32[4,8,64]{2,1,0:T(8,128)} %param.10) | copy-start | bytes 24580
  2.6 7.5 %copy-start = (f32[4,64,56]{1,2,0:T(8,128)S(1)}, f32[4,64,56]{1,2,0:T(8,128)}, u32[]{:S(2)}) copy-start(f32[4,64,56]{1,2,0:T(8,128)} %param.8) | copy-start | bytes 172036
  2.6 16.5 %all-to-all-start = ((bf16[16,64,256]{2,1,0:T(8,128)(2,1)}), bf16[16,64,256]{2,1,0:T(8,128)(2,1)S(1)}, u32[]{:S(2)}, u32[]{:S(2)}) async-start(bf16[16,64,256]{2,1,0:T(8,128)(2,1)} %prepare.1), calls=%async_computation | async-start | bytes 1048576 | tf_op jit(solution)/shard_map/all_to_all | solution.py:473
  10.3 0.7 copy-start.2
  10.3 1.4 %collective-permute-start = (bf16[4,72,64]{2,1,0:T(8,128)(2,1)S(1)}, bf16[4,72,64]{2,1,0:T(8,128)(2,1)S(1)}, u32[]{:S(2)}, u32[]{:S(2)}) collective-permute-start(bf16[4,72,64]{2,1,0:T(8,128)(2,1)S(1)} %fusion.1), channel_id=1, source_target_pairs={{0,128},{128,0},{1,129},{129,1},{2,130},{130,2},{3,131},{131,3},{4... | collective-permute-start | bytes 110600 | tf_op jit(solution)/shard_map/ppermute | solution.py:436
  33.9 1.3 %collective-permute-start.1 = (f32[136,128]{1,0:T(8,128)S(1)}, f32[136,128]{1,0:T(8,128)S(1)}, u32[]{:S(2)}, u32[]{:S(2)}) collective-permute-start(f32[136,128]{1,0:T(8,128)S(1)} %get-tuple-element.25), channel_id=1, source_target_pairs={{0,128},{128,0},{1,129},{129,1},{2,130},{130,2},{3,131},{131,3},{4... | collective-permute-start | bytes 208904 | tf_op jit(solution)/shard_map/ppermute | solution.py:436

commit v7 on v6

--- a/solution.py
+++ b/solution.py
@@ -437,8 +437,10 @@
 
 
 def everyones(block, axis):
-    same = jnp.broadcast_to(block.astype(BF16)[None], (lax.axis_size(axis),) + block.shape)
-    return lax.all_to_all(same, axis, 0, 0, tiled=True)
+    devices = lax.axis_size(axis)
+    same = jnp.broadcast_to(block.astype(BF16)[None], (devices,) + block.shape)
+    groups = [list(reversed(range(devices)))]
+    return lax.all_to_all(same, axis, 0, 0, axis_index_groups=groups, tiled=True)
 
 
 def all_weights(weight_in, bias_in, weight_out, section):

time: 72.5 us -> 70.7 us (0.975)
  blocking collectives: 35.9 us -> 33.8 us
    all_to_all x2, blocking collectives: 35.9 us -> 33.8 us  [everyones(): lax.all_to_all(same, axis, 0, 0, axis_index_groups=groups, tiled=True)]
where the time goes in v7:
time: 70.7 us; the launch traced here: 70 us
  blocking collectives  33.8 us (48%)
  Pallas kernels  19 us (27%)
  starting transfers between devices  7.71 us (11%)
  waiting for transfers between devices  7.49 us (11%)
  local copies, waits for them, and re-layouts  0.95 us (1%)
  between operations  0.76 us (1%)
    all_to_all x2, blocking collectives, everyones(): lax.all_to_all(same, axis, 0, 0, axis_index_groups=groups, tiled=True)  33.8 us
    pallas_call x1, Pallas kernels, rollout(): pl.pallas_call(rollout_kernel, out_shape=(jax.ShapeDtypeStruct((PAIRED *...  14.8 us
    all_to_all x1, starting transfers between devices, body(): received = lax.all_to_all(windows, 'gx', 0, 0, tiled=True)  7.52 us
    all_to_all x1, waiting for transfers between devices, body(): received = lax.all_to_all(windows, 'gx', 0, 0, tiled=True)  5.72 us
    pallas_call x1, Pallas kernels, prepare(): pl.pallas_call(prepare_kernel, out_shape=jax.ShapeDtypeStruct((SLABS, CHU...  1.96 us
    ppermute x2, waiting for transfers between devices, swap(): lax.ppermute(block, axis, [(i, i ^ distance) for i in range(devices)])  1.77 us
    pallas_call x1, Pallas kernels, weave(): pl.pallas_call(weave_kernel, out_shape=(jax.ShapeDtypeStruct((STEPS, 2 *...  1.48 us
  transfers between devices with their start and end apart: 3, of which 3 were waited for; matrix products, arithmetic and copies ran while one was open for 1% of the time, Pallas kernels for 2%

profile of v7, /device:TPU:8, one launch (start us, length us, event | category | flops | bytes accessed | tf_op | source)
XLA Modules:
  0.0 70.0 jit_solution(9290431254853014786)
XLA Ops:
  0.6 2.0 %prepare.1 = bf16[16,64,256]{2,1,0:T(8,128)(2,1)} custom-call(s32[2]{0:T(128)} %order.1, f32[2,256,128]{2,1,0:T(8,128)} %bitcast.9, f32[2,256,128]{2,1,0:T(8,128)} %bitcast.10), custom_call_target="tpu_custom_call" | custom-call | tf_op jit(solution)/shard_map/prepare/pallas_call | solution.py:354
  2.6 0.0 copy-start.1
  2.6 0.0 copy-start
  2.6 7.5 %all-to-all-start = ((bf16[16,64,256]{2,1,0:T(8,128)(2,1)}), bf16[16,64,256]{2,1,0:T(8,128)(2,1)S(1)}, u32[]{:S(2)}, u32[]{:S(2)}) async-start(bf16[16,64,256]{2,1,0:T(8,128)(2,1)} %prepare.1), calls=%async_computation | async-start | bytes 1048576 | tf_op jit(solution)/shard_map/all_to_all | solution.py:475
  10.1 0.0 copy-done.1
  10.1 0.0 copy-done
  10.2 0.1 copy.26
  10.3 0.0 copy-start.2
  10.3 0.1 collective-permute-start
  10.4 0.6 copy-done.2
  11.0 0.1 copy.27
  11.1 0.5 collective-permute-done
  11.7 0.1 maximum_add_fusion
  11.9 1.5 %weave.1 = (bf16[8,144,128]{2,1,0:T(8,128)(2,1)S(1)}, bf16[8,16,128]{2,1,0:T(8,128)(2,1)S(1)}, bf16[8,128,16]{2,1,0:T(8,128)(2,1)S(1)}, bf16[8,112,144]{2,1,0:T(8,128)(2,1)S(1)}) custom-call(f32[8,80,64]{2,1,0:T(8,128)S(1)} %pad.15.weights), custom_call_target="tpu_custom_call" | custom-call | tf_op jit(solution)/shard_map/weave/pallas_call | solution.py:365
  13.4 5.7 %all-to-all-done.received = bf16[16,64,256]{2,1,0:T(8,128)(2,1)S(1)} async-done(((bf16[16,64,256]{2,1,0:T(8,128)(2,1)}), bf16[16,64,256]{2,1,0:T(8,128)(2,1)S(1)}, u32[]{:S(2)}, u32[]{:S(2)}) %all-to-all-start) | async-done | bytes 524320 | tf_op jit(solution)/shard_map/all_to_all | solution.py:475
  19.1 14.8 %rollout.1 = (f32[136,128]{1,0:T(8,128)S(1)}, f32[136,128]{1,0:T(8,128)S(1)}) custom-call(bf16[16,64,256]{2,1,0:T(8,128)(2,1)S(1)} %all-to-all-done.received, bf16[8,144,128]{2,1,0:T(8,128)(2,1)S(1)} %get-tuple-element.20.first, bf16[8,16,128]{2,1,0:T(8,128)(2,1)S(1)} %get-tuple-element.21.second, bf16[8,128,16]{2,1,0:T(8,128)(2,1)S(1)} %get-tuple-element.22.second_back, ...), custom_call_target="tpu_custom_call" | custom-call | tf_op jit(solution)/shard_map/rollout/pallas_call | solution.py:383
  33.9 0.1 collective-permute-start.1
  34.0 1.2 %collective-permute-done.1 = f32[136,128]{1,0:T(8,128)S(1)} collective-permute-done((f32[136,128]{1,0:T(8,128)S(1)}, f32[136,128]{1,0:T(8,128)S(1)}, u32[]{:S(2)}, u32[]{:S(2)}) %collective-permute-start.1) | collective-permute-done | bytes 69664 | tf_op jit(solution)/shard_map/ppermute | solution.py:436
  35.2 0.1 broadcast_in_dim.4
  35.3 16.6 %all_to_all.15 = bf16[16,136,128]{2,1,0:T(8,128)(2,1)S(1)} all-to-all(bf16[16,136,128]{2,1,0:T(8,128)(2,1)S(1)} %broadcast_in_dim.4), channel_id=1, replica_groups={{120,112,104,96,88,80,72,64,56,48,40,32,24,16,8,0},{121,113,105,97,89,8..., dimensions={0} | all-to-all | bytes 1114112 | tf_op jit(solution)/shard_map/all_to_all | solution.py:443
  51.9 0.1 reduce_sum.12
  52.0 17.3 %all_to_all.16.parts = bf16[8,136,128]{2,1,0:T(8,128)(2,1)S(1)} all-to-all(bf16[8,136,128]{2,1,0:T(8,128)(2,1)S(1)} %broadcast_in_dim.5), channel_id=1, replica_groups={{7,6,5,4,3,2,1,0},{15,14,13,12,11,10,9,8},{23,22,21,20,19,18,17,16},{31..., dimensions={0} | all-to-all | bytes 557056 | tf_op jit(solution)/shard_map/all_to_all | solution.py:443
  69.3 0.8 %finish.1 = (f32[4,56,64]{2,1,0:T(8,128)}, f32[4,64]{1,0:T(4,128)}, f32[4,8,64]{2,1,0:T(8,128)}) custom-call(bf16[8,136,128]{2,1,0:T(8,128)(2,1)S(1)} %all_to_all.16.parts), custom_call_target="tpu_custom_call" | custom-call | tf_op jit(solution)/shard_map/finish/pallas_call | solution.py:420
  (9 shorter events, 0.1 us)
Async XLA Ops:
  2.6 7.5 %copy-start.1 = (f32[4,8,64]{2,1,0:T(8,128)S(1)}, f32[4,8,64]{2,1,0:T(8,128)}, u32[]{:S(2)}) copy-start(f32[4,8,64]{2,1,0:T(8,128)} %param.10) | copy-start | bytes 24580
  2.6 7.5 %copy-start = (f32[4,64,56]{1,2,0:T(8,128)S(1)}, f32[4,64,56]{1,2,0:T(8,128)}, u32[]{:S(2)}) copy-start(f32[4,64,56]{1,2,0:T(8,128)} %param.8) | copy-start | bytes 172036
  2.6 16.5 %all-to-all-start = ((bf16[16,64,256]{2,1,0:T(8,128)(2,1)}), bf16[16,64,256]{2,1,0:T(8,128)(2,1)S(1)}, u32[]{:S(2)}, u32[]{:S(2)}) async-start(bf16[16,64,256]{2,1,0:T(8,128)(2,1)} %prepare.1), calls=%async_computation | async-start | bytes 1048576 | tf_op jit(solution)/shard_map/all_to_all | solution.py:475
  10.3 0.7 copy-start.2
  10.3 1.4 %collective-permute-start = (bf16[4,72,64]{2,1,0:T(8,128)(2,1)S(1)}, bf16[4,72,64]{2,1,0:T(8,128)(2,1)S(1)}, u32[]{:S(2)}, u32[]{:S(2)}) collective-permute-start(bf16[4,72,64]{2,1,0:T(8,128)(2,1)S(1)} %fusion.1), channel_id=1, source_target_pairs={{0,128},{128,0},{1,129},{129,1},{2,130},{130,2},{3,131},{131,3},{4... | collective-permute-start | bytes 110600 | tf_op jit(solution)/shard_map/ppermute | solution.py:436
  33.9 1.3 %collective-permute-start.1 = (f32[136,128]{1,0:T(8,128)S(1)}, f32[136,128]{1,0:T(8,128)S(1)}, u32[]{:S(2)}, u32[]{:S(2)}) collective-permute-start(f32[136,128]{1,0:T(8,128)S(1)} %get-tuple-element.25), channel_id=1, source_target_pairs={{0,128},{128,0},{1,129},{129,1},{2,130},{130,2},{3,131},{131,3},{4... | collective-permute-start | bytes 208904 | tf_op jit(solution)/shard_map/ppermute | solution.py:436
